TPU v7x, 256 devices: a whole 4x4x8 slice. The times are simulated.
256 devices in a mesh: section: 8 (over z_lo, core), expert: 8 (over x, z_hi), edata: 4 (over y).
Axes of the slice: x: 4, y: 4, z: 8 (z_hi: 2, z_lo: 4; z = z_hi * 4 + z_lo), core: 2. Of those that a mesh axis runs over, the one named last changes fastest.
Arguments:
- normed_input: bfloat16 [4096, 4096], P(('expert', 'edata'), 'section'), may hold values from -6 to 6
- output_grad: bfloat16 [4096, 4096], P(('expert', 'edata'), 'section'), may hold values from -6 to 6
- expert_ids: int32 [4096, 2], P(('expert', 'edata')), may hold values from 0 to 7, as said below
- slot_pos: int32 [4096, 2], P(('expert', 'edata')), may hold values from 0 to 32, as said below
- router_weight: bfloat16 [4096, 8], replicated, may hold values from -0.09375 to 0.09375
- gate_weight: bfloat16 [8, 7168, 4096], P('expert', ('section', 'edata')), may hold values from -0.09375 to 0.09375
- up_weight: bfloat16 [8, 7168, 4096], P('expert', ('section', 'edata')), may hold values from -0.09375 to 0.09375
- down_weight: bfloat16 [8, 7168, 4096], P('expert', ('section', 'edata')), may hold values from -0.0625 to 0.0625
- saved_gate: bfloat16 [8, 7168, 1024], P('expert', ('section', 'edata')), may hold values from -6 to 6
- saved_up: bfloat16 [8, 7168, 1024], P('expert', ('section', 'edata')), may hold values from -30 to 30
Outputs:
- input_grad: bfloat16 [4096, 4096], P(('expert', 'edata'), 'section')
- grad_router: float32 [4096, 8], P(('section', 'expert', 'edata'))
- grad_gate: bfloat16 [8, 7168, 4096], P('expert', ('section', 'edata'))
- grad_up: bfloat16 [8, 7168, 4096], P('expert', ('section', 'edata'))
- grad_down: bfloat16 [8, 7168, 4096], P('expert', ('section', 'edata'))
Inputs may be any that keep to these rules, and one draw needn't show every extreme that they name: `expert_ids`: the two ids of a token differ. `slot_pos`: within each aligned block of 128 tokens (the tokens of one device), the assignments naming one expert hold distinct positions 0, 1, 2 and so on, in an order drawn for each block; an assignment at position 32 or beyond is dropped and holds 32. In every block some expert fills all 32 positions.
All inputs are finite; a program needn't handle non-finite values.
Results may differ from a plain program's by a relative error of at most 0.02.
Values may be sent and summed in bfloat16 or wider, within the bound.
No kernel may reach another device: no remote copies, remote signals or barrier semaphores. Data moves between devices by JAX's collectives and lax.ppermute only.
A program may use at most 128 MiB of HBM per device.

v0:
```python
import functools

import jax
import jax.numpy as jnp
from jax import lax
from jax.experimental import pallas as pl
from jax.experimental.pallas import tpu as pltpu
from jax.sharding import Mesh, PartitionSpec as P

F32 = jnp.float32
BF16 = jnp.bfloat16
RING = 4
PIECES = 8
LANES = 128
TURN_RIGHT = (((1,), (1,)), ((), ()))
TURN_LEFT = (((0,), (0,)), ((), ()))


def turn(value, axis, step):
    return lax.ppermute(value, axis, [(i, (i + step) % RING) for i in range(RING)])


def swap(value, axis):
    return lax.ppermute(value, axis, [(0, 1), (1, 0)])


def sum_ring(value, axis):
    for bit in (1, 2):
        value = value + lax.ppermute(value, axis, [(i, i ^ bit) for i in range(RING)])
    return value


def sum_turns(value, axis):
    one, two, three = turn(value, axis, 1), turn(value, axis, 2), turn(value, axis, 3)
    return (value + two) + (one + three)


def sum_pair(value, axis):
    return value + swap(value, axis)


def after(value, *others):
    return lax.optimization_barrier((value,) + others)[0]


def params():
    return pltpu.CompilerParams(vmem_limit_bytes=60 * 2**20)


def cost():
    return pl.CostEstimate(flops=1, bytes_accessed=1, transcendentals=0)


def whole_lanes(count):
    return -(-count // LANES) * LANES


def pull_kernel(count, *refs):
    rows, weights, out = refs[:count], refs[count : count + 2], refs[count + 2]
    hidden_dev = weights[0].shape[0]

    @pl.when(pl.program_id(0) == 0)
    def _():
        out[...] = jnp.zeros_like(out)

    left = jnp.concatenate([ref[...] for ref in rows], axis=0)
    for d, weight in enumerate(weights):
        out[d, :, :hidden_dev] += lax.dot_general(left, weight[...], TURN_RIGHT, preferred_element_type=F32)


def pull_call(rows, own, other):
    _, hidden_dev, half = own.shape
    total = sum(r.shape[0] for r in rows)
    step = min(1024, half)
    lanes = whole_lanes(hidden_dev)
    weight = pl.BlockSpec((None, hidden_dev, step), lambda i: (0, 0, i))
    return pl.pallas_call(
        functools.partial(pull_kernel, len(rows)),
        grid=(half // step,),
        in_specs=[pl.BlockSpec((r.shape[0], step), lambda i: (0, i)) for r in rows] + [weight] * 2,
        out_specs=pl.BlockSpec((2, total, lanes), lambda i: (0, 0, 0)),
        out_shape=jax.ShapeDtypeStruct((2, total, lanes), F32),
        compiler_params=params(),
        cost_estimate=cost(),
        name="pull",
    )(*rows, own, other)


def sort_kernel(source, saved, out):
    count, _, total = saved.shape
    pick = (source[...] == lax.broadcasted_iota(jnp.int32, (source.shape[0], total), 1)).astype(BF16)
    for i in range(count):
        out[i] = lax.dot_general(pick, saved[i], TURN_RIGHT, preferred_element_type=F32).astype(BF16)


def sort_call(source, saved):
    count, hidden_dev, total = saved.shape
    block = total // RING
    return pl.pallas_call(
        sort_kernel,
        grid=(RING,),
        in_specs=[
            pl.BlockSpec((block, 1), lambda i: (i, 0)),
            pl.BlockSpec(saved.shape, lambda i: (0, 0, 0)),
        ],
        out_specs=pl.BlockSpec((count, block, hidden_dev), lambda i: (0, i, 0)),
        out_shape=jax.ShapeDtypeStruct((count, total, hidden_dev), BF16),
        compiler_params=params(),
        cost_estimate=cost(),
        name="sort",
    )(source, saved)


def slots_kernel(near, *refs):
    pulls, saved, weights = refs[:4], refs[4], refs[5:9]
    outs, (hidden_out, d_gate, d_up, score, value_ref) = refs[9 : 9 + PIECES], refs[9 + PIECES :]
    step = pl.program_id(0)
    piece, half = outs[0].shape
    hidden_dev = saved.shape[2]
    total, terms = None, []
    for d in range(2):
        near_pull = pulls[0][d] + pulls[1][1 - d]
        far_pull = pulls[2][d] + pulls[3][1 - d]
        pull = jnp.where(step < near, near_pull, far_pull)[:, :hidden_dev]
        pre_gate, pre_up = saved[2 * d].astype(F32), saved[2 * d + 1].astype(F32)
        sigmoid_gate = jax.nn.sigmoid(pre_gate)
        active = pre_gate * sigmoid_gate
        hidden = (active * pre_up).astype(BF16)
        hidden_out[d] = hidden
        point = jnp.sum(hidden.astype(F32) * pull, axis=1, keepdims=True)
        total = point if total is None else total + point
        slope = pre_up * (sigmoid_gate * (1.0 + pre_gate * (1.0 - sigmoid_gate)))
        gate_part = (pull * slope).astype(BF16)
        up_part = (pull * active).astype(BF16)
        d_gate[d] = gate_part
        d_up[d] = up_part
        terms += [(gate_part, weights[2 * d]), (up_part, weights[2 * d + 1])]
    score[...] = total
    run = min(512, half)
    for n in range(0, half, run):
        value = None
        for left, weight in terms:
            term = jnp.dot(left, weight[:, n : n + run], preferred_element_type=F32)
            value = term if value is None else value + term
        value_ref[:, n : n + run] = value.astype(BF16)

    def write(i):
        for j in range(2):
            outs[2 * i + j][...] = value_ref[j * piece : (j + 1) * piece, :]

    for i in range(RING):
        pl.when(step == i)(functools.partial(write, i))


def slots_call(pulls, saved, own, other):
    _, total, hidden_dev = saved.shape
    half = own.shape[2]
    block = total // RING
    near, lanes = pulls[0].shape[1] // block, pulls[0].shape[2]
    shape = jax.ShapeDtypeStruct
    near_spec = pl.BlockSpec((2, block, lanes), lambda i: (0, jnp.minimum(i, near - 1), 0))
    far_spec = pl.BlockSpec((2, block, lanes), lambda i: (0, jnp.maximum(i - near, 0), 0))
    units = pl.BlockSpec((2, block, hidden_dev), lambda i: (0, i, 0))
    four = pl.BlockSpec((4, block, hidden_dev), lambda i: (0, i, 0))
    gate = pl.BlockSpec((None, hidden_dev, half), lambda i: (1, 0, 0))
    up = pl.BlockSpec((None, hidden_dev, half), lambda i: (2, 0, 0))
    out = pl.pallas_call(
        functools.partial(slots_kernel, near),
        grid=(RING,),
        in_specs=[near_spec, near_spec, far_spec, far_spec, four, gate, up, gate, up],
        out_specs=[pl.BlockSpec((block // 2, half), lambda i: (0, 0))] * PIECES
        + [units, units, units, pl.BlockSpec((block, 1), lambda i: (i, 0))],
        out_shape=[shape((block // 2, half), BF16)] * PIECES
        + [shape((2, total, hidden_dev), BF16)] * 3
        + [shape((total, 1), F32)],
        scratch_shapes=[pltpu.VMEM((block, half), BF16)],
        compiler_params=params(),
        cost_estimate=cost(),
        name="slots",
    )(*pulls, saved, own, own, other, other)
    return out[:PIECES], *out[PIECES:]


def arrange_kernel(place, *refs):
    weights, outs = refs[:3], refs[3:]
    features = outs[0].shape[2]

    def copy(core):
        for d, out in enumerate(outs):
            first = (core + d) % 2 * features
            for i, weight in enumerate(weights):
                out[i] = weight[:, first : first + features]

    for core in range(2):
        pl.when(place[RING] == core)(functools.partial(copy, core))


def arrange_call(place, weights, features):
    hidden_dev, width = weights[0].shape
    shape = jax.ShapeDtypeStruct((3, hidden_dev, RING * features), BF16)
    block = (3, hidden_dev, features)
    return pl.pallas_call(
        arrange_kernel,
        grid_spec=pltpu.PrefetchScalarGridSpec(
            num_scalar_prefetch=1,
            grid=(RING,),
            in_specs=[pl.BlockSpec((hidden_dev, 2 * features), lambda r, t: (0, t[r]))] * 3,
            out_specs=[pl.BlockSpec(block, lambda r, t: (0, 0, r))] * 2,
        ),
        out_shape=[shape, shape],
        compiler_params=params(),
        cost_estimate=cost(),
        name="arrange",
    )(place, *weights)


def finish_kernel(place, factor, *refs):
    ins, outs = refs[:6], refs[6:]
    features = ins[0].shape[1]

    def write(core):
        for d in range(2):
            first = (core + d) % 2 * features
            for i, out in enumerate(outs):
                value = factor[0] * ins[2 * i + d][...].astype(F32)
                out[:, first : first + features] = value.astype(BF16)

    for core in range(2):
        pl.when(place[RING] == core)(functools.partial(write, core))


def finish_call(place, factor, pairs, features):
    hidden_dev, half = pairs[0][0].shape
    return pl.pallas_call(
        finish_kernel,
        grid_spec=pltpu.PrefetchScalarGridSpec(
            num_scalar_prefetch=1,
            grid=(RING,),
            in_specs=[pl.BlockSpec(memory_space=pltpu.SMEM)]
            + [pl.BlockSpec((hidden_dev, features), lambda r, t: (0, r))] * 6,
            out_specs=[pl.BlockSpec((None, hidden_dev, 2 * features), lambda r, t: (0, 0, t[r]))] * 3,
        ),
        out_shape=[jax.ShapeDtypeStruct((1, hidden_dev, 2 * half), BF16)] * 3,
        compiler_params=params(),
        cost_estimate=cost(),
        name="finish",
    )(place, factor, *[p for pair in pairs for p in pair])


def grads_kernel(row_count, left_count, gate_count, *refs):
    rows, refs = refs[:row_count], refs[row_count:]
    gates, refs = refs[:gate_count], refs[gate_count:]
    lefts, outs, square = refs[:left_count], refs[left_count : 3 * left_count], refs[3 * left_count]
    turned = refs[3 * left_count + 1]

    @pl.when(pl.program_id(0) == 0)
    def _():
        square[...] = jnp.zeros_like(square)
        for i, left in enumerate(lefts):
            for d in range(2):
                value = left[d].astype(F32)
                if gates:
                    value = value * jnp.concatenate([g[:, 0:1] for g in gates], axis=0).astype(F32)
                turned[2 * i + d] = value.T.astype(BF16)

    right = jnp.concatenate([r[...] for r in rows], axis=0)
    total = jnp.zeros((8, right.shape[1]), F32)
    for i, out in enumerate(outs):
        raw = jnp.dot(turned[i], right, preferred_element_type=F32)
        out[...] = raw.astype(BF16)
        total = total + jnp.sum((raw * raw).reshape(-1, 8, raw.shape[1]), axis=0)
    square[...] += total


def grads_call(rows, gates, lefts, half):
    _, total, hidden_dev = lefts[0].shape
    step = min(512, half)
    shape = jax.ShapeDtypeStruct
    in_specs = [pl.BlockSpec((r.shape[0], step), lambda j: (0, j)) for r in rows]
    in_specs += [pl.BlockSpec((g.shape[0], LANES), lambda j: (0, half // LANES)) for g in gates]
    in_specs += [pl.BlockSpec((2, total, hidden_dev), lambda j: (0, 0, 0))] * len(lefts)
    out = pl.pallas_call(
        functools.partial(grads_kernel, len(rows), len(lefts), len(gates)),
        grid=(half // step,),
        in_specs=in_specs,
        out_specs=[pl.BlockSpec((hidden_dev, step), lambda j: (0, j))] * (2 * len(lefts))
        + [pl.BlockSpec((8, step), lambda j: (0, 0))],
        out_shape=[shape((hidden_dev, half), BF16)] * (2 * len(lefts)) + [shape((8, step), F32)],
        scratch_shapes=[pltpu.VMEM((2 * len(lefts), hidden_dev, total), BF16)],
        compiler_params=params(),
        cost_estimate=cost(),
        name="grads",
    )(*rows, *gates, *lefts)
    return out[0:-1:2], out[1:-1:2], jnp.sum(out[-1])


def local(
    normed_input,
    output_grad,
    expert_ids,
    slot_pos,
    router_weight,
    gate_weight,
    up_weight,
    down_weight,
    saved_gate,
    saved_up,
):
    z, c, x, h, y = (lax.axis_index(name) for name in ("z", "c", "x", "h", "y"))
    width, experts = router_weight.shape
    tokens, features = normed_input.shape
    hidden_dev = gate_weight.shape[1]
    slot_total = saved_gate.shape[2]
    capacity = slot_total // (8 * RING)
    piece = RING * capacity
    block = 2 * piece
    half = RING * features

    near_expert = ((expert_ids % 2 + h) % 2) * RING + (expert_ids // 2 - x) % RING
    live_mask = slot_pos < capacity
    address = near_expert * capacity + slot_pos
    table = jnp.arange(block, dtype=jnp.int32)[None, :]
    first_pick = (address[:, 0:1] == table) & live_mask[:, 0:1]
    second_pick = (address[:, 1:2] == table) & live_mask[:, 1:2]
    pick_matrix = (first_pick | second_pick).astype(BF16)

    def place(matrix, values):
        return lax.dot_general(matrix, values, TURN_LEFT, preferred_element_type=F32).astype(BF16)

    def exchange_x(rows, sign):
        parts = rows.reshape(2, RING, capacity, -1)
        out = [parts[:, 0]] + [turn(parts[:, a], "x", sign * a) for a in range(1, RING)]
        return [jnp.concatenate([part[b] for part in out], axis=0) for b in range(2)]

    def gather_z(rows):
        return jnp.concatenate([rows] + [turn(rows, "z", r) for r in range(1, RING)], axis=1)

    def add(*terms):
        return functools.reduce(lambda a, b: a + b, [t.astype(F32) for t in terms])

    barrier = lax.optimization_barrier

    def spread_x(rows):
        parts = [rows[a * capacity : (a + 1) * capacity] for a in range(RING)]
        return jnp.concatenate(parts[:1] + [turn(parts[a], "x", a) for a in range(1, RING)], axis=0)

    dy_placed = place(pick_matrix, output_grad)
    near, far = dy_placed[:piece], dy_placed[piece:]
    far = swap(far, "h")
    near = spread_x(near)
    router_rows = lax.dynamic_slice_in_dim(router_weight, (z * 2 + c) * features, features, 0)
    logits = jnp.dot(normed_input, router_rows, preferred_element_type=F32)
    logits = sum_pair(after(logits, dy_placed), "c")
    sections = jnp.stack([(z - r) % RING for r in range(RING)] + [c]).astype(jnp.int32)
    weights = after((down_weight[0], gate_weight[0], up_weight[0]), dy_placed)
    own_weights, other_weights = arrange_call(sections, weights, features)
    near, far, logits, own_weights, other_weights = barrier((near, far, logits, own_weights, other_weights))

    near = gather_z(near)
    logits = sum_ring(logits, "z")
    far = spread_x(far)
    columns = jnp.arange(experts, dtype=jnp.int32)[None, :]
    first_hot = (columns == expert_ids[:, 0:1]).astype(F32)
    second_hot = (columns == expert_ids[:, 1:2]).astype(F32)
    pair_hot = first_hot - second_hot
    first_share = jax.nn.sigmoid(
        jnp.sum(logits * first_hot, axis=1) - jnp.sum(logits * second_hot, axis=1)
    )
    gate_first = first_share.astype(BF16).astype(F32)
    gate_second = (1.0 - first_share).astype(BF16).astype(F32)
    gate_matrix = jnp.where(first_pick, gate_first[:, None], 0.0) + jnp.where(
        second_pick, gate_second[:, None], 0.0
    )
    gated = jnp.concatenate([normed_input, jnp.ones((tokens, LANES), BF16)], axis=1)
    x_placed = place(gate_matrix.astype(BF16), gated)
    near, far, x_placed = barrier((near, far, x_placed))

    near_left, near_right = turn(near, "y", 1), turn(near, "y", -1)
    far = gather_z(far)
    x_near, x_far = exchange_x(x_placed, 1)
    other_weights = swap(after(other_weights, near), "c")
    saved = after(jnp.concatenate([saved_gate, saved_up], axis=0), near)
    saved = jnp.concatenate([saved, swap(saved, "c")], axis=0)
    far, x_near, x_far, saved, other_weights = barrier((far, x_near, x_far, saved, other_weights))

    far_left, far_right = turn(far, "y", 1), turn(far, "y", -1)
    x_far = swap(x_far, "h")
    x_near_z = gather_z(x_near[:, :features])
    order = jnp.arange(slot_total, dtype=jnp.int32)
    turn_y = order // block
    from_y = (y + jnp.where(turn_y < 2, turn_y, 5 - turn_y)) % RING
    from_h = (h + (order // piece) % 2) % 2
    from_x = (x - (order // capacity) % RING) % RING
    source = ((from_x * 2 + from_h) * RING + from_y) * capacity + order % capacity
    saved = sort_call(source[:, None], saved)
    near_left, near_right, x_far, x_near = barrier((near_left, near_right, x_far, x_near))
    near_across = turn(near_left, "y", 1)
    x_far_z = gather_z(x_far[:, :features])
    far_left, far_right, saved = barrier((far_left, far_right, saved))

    far_across = turn(far_right, "y", -1)
    dy_pieces = [near, far, near_right, far_right, near_left, far_left]
    near_pull = pull_call(dy_pieces, own_weights, other_weights)
    near_across, far_across, x_near_z, x_far_z = barrier((near_across, far_across, x_near_z, x_far_z))
    across = [near_across, far_across]
    x_rows = jnp.concatenate(
        [
            jnp.concatenate([x_near_z, x_near[:, features:]], axis=1),
            jnp.concatenate([x_far_z, x_far[:, features:]], axis=1),
        ],
        axis=0,
    )

    x_left, x_right = turn(x_rows, "y", 1), turn(x_rows, "y", -1)
    far_pull = pull_call(across, own_weights, other_weights)
    pulls = [near_pull, swap(near_pull, "c"), far_pull, swap(far_pull, "c")]
    dx, hidden, d_gate, d_up, score = slots_call(pulls, saved, own_weights, other_weights)

    from_left, from_right = turn(dx[6], "y", 1), turn(dx[7], "y", -1)
    score = score.reshape(RING, block)
    scores = [turn(score[1], "y", 1), turn(score[2], "y", -1), turn(score[3], "y", 2)]
    from_left, from_right, x_left, x_right = barrier((from_left, from_right, x_left, x_right))

    to_right = add(dx[2], from_left).astype(BF16)
    to_left = add(dx[5], from_right).astype(BF16)
    moved = [
        (turn(right, "y", 1), turn(left, "y", -1))
        for right, left in ((dx[3], to_left), (to_right, dx[4]))
    ]
    scores = after(scores, to_left, to_right)
    score = sum_ring(score[0] + scores[0] + scores[1] + scores[2], "z").reshape(2, RING, capacity)
    moved[0], score, x_left, x_right = barrier((moved[0], score, x_left, x_right))

    x_across = turn(x_left[:piece], "y", 1), turn(x_right[piece:], "y", -1)
    sums = [add(dx[1 - i], *pair).astype(BF16) for i, pair in enumerate(moved)]

    def turn_z(own):
        return [turn(own[:, r * features : (r + 1) * features], "z", -r) for r in range(1, RING)]

    parts = [turn_z(sums[0]), None]
    score = jnp.stack([score[0], swap(score[1], "h")])
    score = [score[:, 0]] + [turn(score[:, a], "x", -a) for a in range(1, RING)]
    score = jnp.stack(score, axis=1).reshape(1, block)
    parts[0], x_across, score = barrier((parts[0], x_across, score))
    far = add(sums[0][:, :features], *parts[0]).astype(BF16)
    x_pieces = [x_rows, x_right, x_left, *x_across]
    own_two, other_two, two_square = grads_call(x_pieces, [], [d_gate, d_up], half)
    sums[1], hidden = after((sums[1], hidden), two_square)
    parts[1] = turn_z(sums[1])
    (own_down,), (other_down,), down_square = grads_call(dy_pieces + across, x_pieces, [hidden], half)
    first_grad = jnp.sum(jnp.where(first_pick, score, 0.0), axis=1)
    second_grad = jnp.sum(jnp.where(second_pick, score, 0.0), axis=1)
    logit_step = (first_grad - second_grad) * first_share * (1.0 - first_share)
    logit_grad = pair_hot * logit_step[:, None]
    router_term = lax.dot_general(
        logit_grad, normed_input.astype(F32), TURN_LEFT, precision=lax.Precision.HIGHEST
    )
    parts[1], router_term, two_square, down_square = barrier(
        (parts[1], router_term, two_square, down_square)
    )
    near = add(sums[1][:, :features], *parts[1]).astype(BF16)

    far = swap(far, "h")
    message = jnp.concatenate(
        [router_term, jnp.full((8, features), down_square + two_square, F32)], axis=0
    )
    message = sum_turns(message, "y")
    far, message = barrier((far, message))
    back_dx = exchange_x(jnp.concatenate([near, far], axis=0), -1)
    message = sum_turns(message, "x")
    back_dx, message = barrier((back_dx, message))
    other_down = swap(other_down, "c")
    other_two = [swap(part, "c") for part in other_two]
    message = sum_pair(message, "h")
    raw_router = message[:experts]
    square_sum = jnp.full((8, LANES), message[experts, 0] + jnp.sum(raw_router * raw_router), F32)
    square_sum = sum_turns(sum_pair(square_sum, "c"), "z")[0, 0]
    row_count = features // (8 * RING)
    raw_router = lax.dynamic_slice_in_dim(
        raw_router, ((x * 2 + h) * RING + y) * row_count, row_count, 1
    ).T
    back_dx = jnp.concatenate(back_dx, axis=0)
    token_dx = jnp.dot(gate_matrix, back_dx.astype(F32), precision=lax.Precision.HIGHEST)
    input_grad = (
        token_dx
        + lax.dot_general(
            logit_grad, router_rows.astype(F32), TURN_RIGHT, precision=lax.Precision.HIGHEST
        )
    ).astype(BF16)
    entry_count = 3.0 * experts * hidden_dev * 8 * RING * width + 1.0 * width * experts
    factor = 1.0 / jnp.maximum(jnp.sqrt(square_sum / entry_count), 1.0)
    pairs = [(own_two[0], other_two[0]), (own_two[1], other_two[1]), (own_down, other_down)]
    grad_gate, grad_up, grad_down = finish_call(sections, factor.reshape(1), pairs, features)
    return (input_grad, factor * raw_router, grad_gate, grad_up, grad_down)


def solution(mesh):
    fine = Mesh(mesh.devices.reshape(4, 2, 4, 2, 4), ("z", "c", "x", "h", "y"))
    section, expert, edata = ("z", "c"), ("x", "h"), "y"
    rows = P((*expert, edata), section)
    ids = P((*expert, edata), None)
    weight = P(expert, (*section, edata), None)
    in_specs = (rows, rows, ids, ids, P(), weight, weight, weight, weight, weight)
    out_specs = (rows, P((*section, *expert, edata), None), weight, weight, weight)
    return jax.shard_map(local, mesh=fine, in_specs=in_specs, out_specs=out_specs, check_vma=False)
```

profile of v0, /device:TPU:6, one launch (start us, length us, event | category | flops | bytes accessed | tf_op | source)
XLA Modules:
  0.0 290.0 jit_solution(12367296357226395318)
XLA Ops:
  3.4 2.8 collective-permute-start.1
  6.7 7.3 %collective-permute-start.3 = (bf16[128,512]{1,0:T(8,128)(2,1)S(1)}, bf16[128,512]{1,0:T(8,128)(2,1)S(1)}, u32[]{:S(2)}, u32[]{:S(2)}) collective-permute-start(bf16[128,512]{1,0:T(8,128)(2,1)S(1)} %slice.279), channel_id=1, source_target_pairs={{0,4},{4,0},{1,5},{5,1},{2,6},{6,2},{3,7},{7,3},{8,12},{12,8},{9,1... | collective-permute-start | bytes 393224 | tf_op jit(solution)/shard_map/ppermute | solution.py:24
  15.7 6.3 %arrange.1 = (bf16[3,224,2048]{2,1,0:T(8,128)(2,1)}, bf16[3,224,2048]{2,1,0:T(8,128)(2,1)}) custom-call(s32[5]{0:T(128)} %stack.41.place, bf16[224,4096]{1,0:T(8,128)(2,1)} %bitcast.104, bf16[224,4096]{1,0:T(8,128)(2,1)} %bitcast.105, bf16[224,4096]{1,0:T(8,128)(2,1)} %bitcast.106), custom_call_target="tpu_custom_call" | custom-call | flops 1 | bytes 1 | tf_op jit(solution)/shard_map/arrange/pallas_call | solution.py:202
  23.1 1.9 collective-permute-start.9
  26.7 1.5 collective-permute-start.6
  28.3 9.5 %collective-permute-done.6 = f32[128,8]{0,1:T(8,128)S(1)} collective-permute-done((f32[128,8]{0,1:T(8,128)S(1)}, f32[128,8]{0,1:T(8,128)S(1)}, u32[]{:S(2)}, u32[]{:S(2)}) %collective-permute-start.6) | collective-permute-done | bytes 4128 | tf_op jit(solution)/shard_map/ppermute | solution.py:29
  37.8 2.1 collective-permute-start.11
  41.1 2.1 collective-permute-done.11
  44.3 3.2 %collective-permute-start.15 = (bf16[128,512]{1,0:T(8,128)(2,1)S(1)}, bf16[128,512]{1,0:T(8,128)(2,1)S(1)}, u32[]{:S(2)}, u32[]{:S(2)}) collective-permute-start(bf16[128,512]{1,0:T(8,128)(2,1)S(1)} %pad_maximum_fusion.10), channel_id=1, source_target_pairs={{0,192},{64,0},{128,64},{192,128},{1,193},{65,1},{129,65},{193,129... | collective-permute-start | bytes 393224 | tf_op jit(solution)/shard_map/ppermute | solution.py:20
  47.9 3.3 %collective-permute-start.17 = (bf16[2,32,640]{2,1,0:T(8,128)(2,1)S(1)}, bf16[2,32,640]{2,1,0:T(8,128)(2,1)S(1)}, u32[]{:S(2)}, u32[]{:S(2)}) collective-permute-start(bf16[2,32,640]{2,1,0:T(8,128)(2,1)S(1)} %get-tuple-element.196), channel_id=1, source_target_pairs={{0,16},{8,24},{16,0},{24,8},{1,17},{9,25},{17,1},{25,9},{2,18},{10... | collective-permute-start | bytes 245768 | tf_op jit(solution)/shard_map/ppermute | solution.py:20
  51.3 3.1 %collective-permute-done.18 = bf16[2,32,640]{2,1,0:T(8,128)(2,1)S(1)} collective-permute-done((bf16[2,32,640]{2,1,0:T(8,128)(2,1)S(1)}, bf16[2,32,640]{2,1,0:T(8,128)(2,1)S(1)}, u32[]{:S(2)}, u32[]{:S(2)}) %collective-permute-start.18) | collective-permute-done | bytes 81952 | tf_op jit(solution)/shard_map/ppermute | solution.py:20
  55.5 1.7 collective-permute-start.16
  57.2 2.7 collective-permute-done.16
  61.3 1.6 collective-permute-start.21
  62.9 1.7 collective-permute-start.22
  64.6 2.1 collective-permute-done.13
  69.0 1.6 collective-permute-start.24
  70.5 1.7 collective-permute-start.25
  74.3 3.3 %collective-permute-done.21.refs_4_ = bf16[128,2048]{1,0:T(8,128)(2,1)} collective-permute-done((bf16[128,2048]{1,0:T(8,128)(2,1)S(1)}, bf16[128,2048]{1,0:T(8,128)(2,1)}, u32[]{:S(2)}, u32[]{:S(2)}) %collective-permute-start.21) | collective-permute-done | bytes 524320 | tf_op jit(solution)/shard_map/ppermute | solution.py:20
  77.5 2.0 collective-permute-start.30
  79.5 1.4 collective-permute-start.23
  81.0 1.6 fusion.15.source
  82.6 5.9 %sort.1.refs_4_ = bf16[4,1024,224]{2,1,0:T(8,128)(2,1)} custom-call(s32[1024,1]{1,0:T(8,128)} %fusion.15.source, bf16[4,224,1024]{2,1,0:T(8,128)(2,1)} %pad_maximum_fusion.saved), custom_call_target="tpu_custom_call" | custom-call | flops 1 | bytes 1 | tf_op jit(solution)/shard_map/sort/pallas_call | solution.py:99
  88.5 1.8 collective-permute-done.23
  90.3 4.9 %pull.2.refs_0_ = f32[2,768,256]{2,1,0:T(8,128)} custom-call(bf16[128,2048]{1,0:T(8,128)(2,1)} %copy-done.6, bf16[128,2048]{1,0:T(8,128)(2,1)} %pad_maximum_fusion.3.refs_1_, bf16[128,2048]{1,0:T(8,128)(2,1)} %collective-permute-done.22.refs_2_, bf16[128,2048]{1,0:T(8,128)(2,1)} %collective-permute-done.25.refs_3_, ...), custom_call_target="tpu_custom_call" | custom-call | flops 1 | bytes 1 | tf_op jit(solution)/shard_map/pull/pallas_call | solution.py:77
  95.3 2.7 collective-permute-start.29
  97.9 10.2 %collective-permute-start.34 = (bf16[128,512]{1,0:T(8,128)(2,1)S(1)}, bf16[128,512]{1,0:T(8,128)(2,1)S(1)}, u32[]{:S(2)}, u32[]{:S(2)}) collective-permute-start(bf16[128,512]{1,0:T(8,128)(2,1)S(1)} %slice.238), channel_id=1, source_target_pairs={{0,192},{64,0},{128,64},{192,128},{1,193},{65,1},{129,65},{193,129... | collective-permute-start | bytes 393224 | tf_op jit(solution)/shard_map/ppermute | solution.py:20
  108.5 2.9 collective-permute-start.28
  114.6 8.1 %collective-permute-done.33 = bf16[128,512]{1,0:T(8,128)(2,1)S(1)} collective-permute-done((bf16[128,512]{1,0:T(8,128)(2,1)S(1)}, bf16[128,512]{1,0:T(8,128)(2,1)S(1)}, u32[]{:S(2)}, u32[]{:S(2)}) %collective-permute-start.33) | collective-permute-done | bytes 131104 | tf_op jit(solution)/shard_map/ppermute | solution.py:20
  123.9 2.8 collective-permute-start.39
  126.7 3.1 %pull.3.refs_2_ = f32[2,256,256]{2,1,0:T(8,128)} custom-call(bf16[128,2048]{1,0:T(8,128)(2,1)} %copy-done.9, bf16[128,2048]{1,0:T(8,128)(2,1)} %collective-permute-done.28.refs_1_.refs_7_, bf16[3,224,2048]{2,1,0:T(8,128)(2,1)} %get-tuple-element.114.refs_6_.refs_2_.refs_5_, bf16[3,224,2048]{2,1,0:T(8,128)(2,1)} %copy-done.2), custom_call_target="tpu_custom_call" | custom-call | flops 1 | bytes 1 | tf_op jit(solution)/shard_map/pull/pallas_call | solution.py:77
  129.8 2.1 collective-permute-done.35.refs_3_
  132.8 11.5 %slots.1 = (bf16[128,2048]{1,0:T(8,128)(2,1)}, bf16[128,2048]{1,0:T(8,128)(2,1)}, bf16[128,2048]{1,0:T(8,128)(2,1)}, bf16[128,2048]{1,0:T(8,128)(2,1)}, bf16[128...) custom-call(f32[2,768,256]{2,1,0:T(8,128)} %pull.2.refs_0_, ...), custom_call_target="tpu_custom_call" | custom-call | flops 1 | bytes 1 | tf_op jit(solution)/shard_map/slots/pallas_call | solution.py:167
  144.3 3.2 %collective-permute-start.37 = (bf16[128,2048]{1,0:T(8,128)(2,1)}, bf16[128,2048]{1,0:T(8,128)(2,1)S(1)}, u32[]{:S(2)}, u32[]{:S(2)}) collective-permute-start(bf16[128,2048]{1,0:T(8,128)(2,1)} %get-tuple-element.123), channel_id=1, source_target_pairs={{0,3},{1,0},{2,1},{3,2},{4,7},{5,4},{6,5},{7,6},{8,11},{9,8},{10,9... | collective-permute-start | bytes 1572872 | tf_op jit(solution)/shard_map/ppermute | solution.py:20
  148.9 3.3 %collective-permute-done.38.refs_2_.refs_10_ = bf16[256,2176]{1,0:T(8,128)(2,1)S(1)} collective-permute-done((bf16[256,2176]{1,0:T(8,128)(2,1)S(1)}, bf16[256,2176]{1,0:T(8,128)(2,1)S(1)}, u32[]{:S(2)}, u32[]{:S(2)}) %collective-permute-start.38) | collective-permute-done | bytes 1114144 | tf_op jit(solution)/shard_map/ppermute | solution.py:20
  152.2 3.2 %collective-permute-start.45 = (f32[256]{0:T(256)S(1)}, f32[256]{0:T(256)S(1)}, u32[]{:S(2)}, u32[]{:S(2)}) collective-permute-start(f32[256]{0:T(256)S(1)} %get-tuple-element.179), channel_id=1, source_target_pairs={{0,3},{1,0},{2,1},{3,2},{4,7},{5,4},{6,5},{7,6},{8,11},{9,8},{10,9... | collective-permute-start | bytes 3080 | tf_op jit(solution)/shard_map/ppermute | solution.py:20
  155.5 8.0 %collective-permute-done.36 = bf16[128,2048]{1,0:T(8,128)(2,1)S(1)} collective-permute-done((bf16[128,2048]{1,0:T(8,128)(2,1)}, bf16[128,2048]{1,0:T(8,128)(2,1)S(1)}, u32[]{:S(2)}, u32[]{:S(2)}) %collective-permute-start.36) | collective-permute-done | bytes 524320 | tf_op jit(solution)/shard_map/ppermute | solution.py:20
  167.9 5.1 %collective-permute-done.44 = f32[256]{0:T(256)S(1)} collective-permute-done((f32[256]{0:T(256)S(1)}, f32[256]{0:T(256)S(1)}, u32[]{:S(2)}, u32[]{:S(2)}) %collective-permute-start.44) | collective-permute-done | bytes 1056 | tf_op jit(solution)/shard_map/ppermute | solution.py:20
  174.5 2.8 collective-permute-done.47
  180.1 1.6 collective-permute-done.48
  181.8 2.8 collective-permute-start.54
  184.6 1.6 add_convert_fusion
  189.6 3.1 %collective-permute-start.57 = (f32[2,32]{1,0:T(2,128)S(1)}, f32[2,32]{1,0:T(2,128)S(1)}, u32[]{:S(2)}, u32[]{:S(2)}) collective-permute-start(f32[2,32]{1,0:T(2,128)S(1)} %bitcast.118), channel_id=1, source_target_pairs={{0,8},{8,16},{16,24},{24,0},{1,9},{9,17},{17,25},{25,1},{2,10},{10... | collective-permute-start | bytes 776 | tf_op jit(solution)/shard_map/ppermute | solution.py:20
  195.0 2.7 collective-permute-done.56
  197.8 3.2 %collective-permute-start.53 = (bf16[128,2176]{1,0:T(8,128)(2,1)S(1)}, bf16[128,2176]{1,0:T(8,128)(2,1)S(1)}, u32[]{:S(2)}, u32[]{:S(2)}) collective-permute-start(bf16[128,2176]{1,0:T(8,128)(2,1)S(1)} %slice.249), channel_id=1, source_target_pairs={{0,3},{1,0},{2,1},{3,2},{4,7},{5,4},{6,5},{7,6},{8,11},{9,8},{10,9... | collective-permute-start | bytes 1671176 | tf_op jit(solution)/shard_map/ppermute | solution.py:20
  202.4 6.3 %collective-permute-done.52.refs_3_.refs_11_ = bf16[128,2176]{1,0:T(8,128)(2,1)S(1)} collective-permute-done((bf16[128,2176]{1,0:T(8,128)(2,1)}, bf16[128,2176]{1,0:T(8,128)(2,1)S(1)}, u32[]{:S(2)}, u32[]{:S(2)}) %collective-permute-start.52) | collective-permute-done | bytes 557088 | tf_op jit(solution)/shard_map/ppermute | solution.py:20
  210.2 3.0 %collective-permute-start.61 = (bf16[128,512]{1,0:T(8,128)(2,1)S(1)}, bf16[128,512]{1,0:T(8,128)(2,1)S(1)}, u32[]{:S(2)}, u32[]{:S(2)}) collective-permute-start(bf16[128,512]{1,0:T(8,128)(2,1)S(1)} %add_convert_fusion.4), channel_id=1, source_target_pairs={{0,4},{4,0},{1,5},{5,1},{2,6},{6,2},{3,7},{7,3},{8,12},{12,8},{9,1... | collective-permute-start | bytes 393224 | tf_op jit(solution)/shard_map/ppermute | solution.py:24
  213.1 8.0 %grads.2 = (bf16[224,2048]{1,0:T(8,128)(2,1)}, bf16[224,2048]{1,0:T(8,128)(2,1)}, bf16[224,2048]{1,0:T(8,128)(2,1)}, bf16[224,2048]{1,0:T(8,128)(2,1)}, f32[8,512]{1,0:T(8,128)}) custom-call(bf16[256,2176]{1,0:T(8,128)(2,1)} %copy-done.3, bf16[256,2176]{1,0:T(8,128)(2,1)} %copy-done.5, bf16[256,2176]{1,0:T(8,128)(2,1)} %copy-done.4, ...), custom_call_target="tpu_custom_call" | custom-call | flops 1 | bytes 1 | tf_op jit(solution)/shard_map/grads/pallas_call | solution.py:282
  221.1 1.4 reduce_sum.65
  222.6 2.9 %collective-permute-start.58 = (bf16[128,512]{1,0:T(8,128)(2,1)S(1)}, bf16[128,512]{1,0:T(8,128)(2,1)S(1)}, u32[]{:S(2)}, u32[]{:S(2)}) collective-permute-start(bf16[128,512]{1,0:T(8,128)(2,1)S(1)} %get-tuple-element.189), channel_id=1, source_target_pairs={{0,192},{64,0},{128,64},{192,128},{1,193},{65,1},{129,65},{193,129... | collective-permute-start | bytes 393224 | tf_op jit(solution)/shard_map/ppermute | solution.py:20
  225.5 1.7 collective-permute-start.60
  227.2 6.6 %grads.3 = (bf16[224,2048]{1,0:T(8,128)(2,1)}, bf16[224,2048]{1,0:T(8,128)(2,1)}, f32[8,512]{1,0:T(8,128)}) custom-call(bf16[128,2048]{1,0:T(8,128)(2,1)} %copy-done.6, bf16[128,2048]{1,0:T(8,128)(2,1)} %pad_maximum_fusion.3.refs_1_, bf16[128,2048]{1,0:T(8,128)(2,1)} %collective-permute-done.22.refs_2_, bf16[128,2048]{1,0:T(8,128)(2,1)} %collective-permute-done.25.refs_3_, ...), custom_call_target="tpu_custom_call" | custom-call | flops 1 | bytes 1 | tf_op jit(solution)/shard_map/grads/pallas_call | solution.py:282
  236.9 3.2 %collective-permute-start.64 = (f32[16,512]{1,0:T(8,128)S(1)}, f32[16,512]{1,0:T(8,128)S(1)}, u32[]{:S(2)}, u32[]{:S(2)}) collective-permute-start(f32[16,512]{1,0:T(8,128)S(1)} %concatenate.71), channel_id=1, source_target_pairs={{0,3},{1,0},{2,1},{3,2},{4,7},{5,4},{6,5},{7,6},{8,11},{9,8},{10,9... | collective-permute-start | bytes 98312 | tf_op jit(solution)/shard_map/ppermute | solution.py:20
  242.0 3.5 %collective-permute-done.62 = f32[16,512]{1,0:T(8,128)S(1)} collective-permute-done((f32[16,512]{1,0:T(8,128)S(1)}, f32[16,512]{1,0:T(8,128)S(1)}, u32[]{:S(2)}, u32[]{:S(2)}) %collective-permute-start.62) | collective-permute-done | bytes 32800 | tf_op jit(solution)/shard_map/ppermute | solution.py:20
  248.1 2.3 collective-permute-start.67
  250.5 2.1 collective-permute-start.66
  253.1 3.1 %collective-permute-done.66 = bf16[2,32,512]{2,1,0:T(8,128)(2,1)S(1)} collective-permute-done((bf16[2,32,512]{2,1,0:T(8,128)(2,1)S(1)}, bf16[2,32,512]{2,1,0:T(8,128)(2,1)S(1)}, u32[]{:S(2)}, u32[]{:S(2)}) %collective-permute-start.66) | collective-permute-done | bytes 65568 | tf_op jit(solution)/shard_map/ppermute | solution.py:20
  256.2 1.8 collective-permute-done.65
  258.1 3.4 %collective-permute-start.71 = (f32[16,512]{1,0:T(8,128)S(1)}, f32[16,512]{1,0:T(8,128)S(1)}, u32[]{:S(2)}, u32[]{:S(2)}) collective-permute-start(f32[16,512]{1,0:T(8,128)S(1)} %add_add_fusion), channel_id=1, source_target_pairs={{0,4},{4,0},{1,5},{5,1},{2,6},{6,2},{3,7},{7,3},{8,12},{12,8},{9,1... | collective-permute-start | bytes 98312 | tf_op jit(solution)/shard_map/ppermute | solution.py:24
  261.5 4.5 %collective-permute-done.71 = f32[16,512]{1,0:T(8,128)S(1)} collective-permute-done((f32[16,512]{1,0:T(8,128)S(1)}, f32[16,512]{1,0:T(8,128)S(1)}, u32[]{:S(2)}, u32[]{:S(2)}) %collective-permute-start.71) | collective-permute-done | bytes 32800 | tf_op jit(solution)/shard_map/ppermute | solution.py:24
  269.7 2.3 collective-permute-start.74
  272.9 1.8 collective-permute-start.75
  276.6 3.1 %collective-permute-done.73 = f32[8,128]{1,0:T(8,128)S(1)} collective-permute-done((f32[8,128]{1,0:T(8,128)S(1)}, f32[8,128]{1,0:T(8,128)S(1)}, u32[]{:S(2)}, u32[]{:S(2)}) %collective-permute-start.73) | collective-permute-done | bytes 4128 | tf_op jit(solution)/shard_map/ppermute | solution.py:20
  283.2 6.5 %finish.1 = (bf16[1,224,4096]{2,1,0:T(8,128)(2,1)}, bf16[1,224,4096]{2,1,0:T(8,128)(2,1)}, bf16[1,224,4096]{2,1,0:T(8,128)(2,1)}) custom-call(s32[5]{0:T(128)} %stack.41.place, f32[1]{0:T(128)} %bitcast.54.factor, bf16[224,2048]{1,0:T(8,128)(2,1)} %get-tuple-element.168.refs_0_, bf16[224,2048]{1,0:T(8,128)(2,1)} %copy-done.10, ...), custom_call_target="tpu_custom_call" | custom-call | flops 1 | bytes 1 | tf_op jit(solution)/shard_map/finish/pallas_call | solution.py:234
  (250 shorter events, 56.1 us)
Async XLA Ops:
  2.5 19.4 %collective-permute-start.2 = (bf16[32,512]{1,0:T(8,128)(2,1)S(1)}, bf16[32,512]{1,0:T(8,128)(2,1)S(1)}, u32[]{:S(2)}, u32[]{:S(2)}) collective-permute-start(bf16[32,512]{1,0:T(8,128)(2,1)S(1)} %get-tuple-element.204), channel_id=1, source_target_pairs={{0,24},{8,0},{16,8},{24,16},{1,25},{9,1},{17,9},{25,17},{2,26},{10... | collective-permute-start | bytes 98312 | tf_op jit(solution)/shard_map/ppermute | solution.py:20
  3.4 18.5 %collective-permute-start.1 = (bf16[32,512]{1,0:T(8,128)(2,1)S(1)}, bf16[32,512]{1,0:T(8,128)(2,1)S(1)}, u32[]{:S(2)}, u32[]{:S(2)}) collective-permute-start(bf16[32,512]{1,0:T(8,128)(2,1)S(1)} %get-tuple-element.205), channel_id=1, source_target_pairs={{0,16},{8,24},{16,0},{24,8},{1,17},{9,25},{17,1},{25,9},{2,18},{10... | collective-permute-start | bytes 98312 | tf_op jit(solution)/shard_map/ppermute | solution.py:20
  6.3 15.7 %collective-permute-start = (bf16[32,512]{1,0:T(8,128)(2,1)S(1)}, bf16[32,512]{1,0:T(8,128)(2,1)S(1)}, u32[]{:S(2)}, u32[]{:S(2)}) collective-permute-start(bf16[32,512]{1,0:T(8,128)(2,1)S(1)} %get-tuple-element.206), channel_id=1, source_target_pairs={{0,8},{8,16},{16,24},{24,0},{1,9},{9,17},{17,25},{25,1},{2,10},{10... | collective-permute-start | bytes 98312 | tf_op jit(solution)/shard_map/ppermute | solution.py:20
  6.7 15.4 %collective-permute-start.3 = (bf16[128,512]{1,0:T(8,128)(2,1)S(1)}, bf16[128,512]{1,0:T(8,128)(2,1)S(1)}, u32[]{:S(2)}, u32[]{:S(2)}) collective-permute-start(bf16[128,512]{1,0:T(8,128)(2,1)S(1)} %slice.279), channel_id=1, source_target_pairs={{0,4},{4,0},{1,5},{5,1},{2,6},{6,2},{3,7},{7,3},{8,12},{12,8},{9,1... | collective-permute-start | bytes 393224 | tf_op jit(solution)/shard_map/ppermute | solution.py:24
  15.0 7.0 %collective-permute-start.4 = (f32[128,8]{0,1:T(8,128)S(1)}, f32[128,8]{0,1:T(8,128)S(1)}, u32[]{:S(2)}, u32[]{:S(2)}) collective-permute-start(f32[128,8]{0,1:T(8,128)S(1)} %convolution_bitcast_fusion), channel_id=1, source_target_pairs={{0,32},{32,0},{1,33},{33,1},{2,34},{34,2},{3,35},{35,3},{4,36},{36... | collective-permute-start | bytes 12296 | tf_op jit(solution)/shard_map/ppermute | solution.py:24
  23.1 20.8 %collective-permute-start.9 = (bf16[128,512]{1,0:T(8,128)(2,1)S(1)}, bf16[128,512]{1,0:T(8,128)(2,1)S(1)}, u32[]{:S(2)}, u32[]{:S(2)}) collective-permute-start(bf16[128,512]{1,0:T(8,128)(2,1)S(1)} %pad_maximum_fusion.9), channel_id=1, source_target_pairs={{0,192},{64,0},{128,64},{192,128},{1,193},{65,1},{129,65},{193,129... | collective-permute-start | bytes 393224 | tf_op jit(solution)/shard_map/ppermute | solution.py:20
  25.1 18.9 %collective-permute-start.8 = (bf16[128,512]{1,0:T(8,128)(2,1)S(1)}, bf16[128,512]{1,0:T(8,128)(2,1)S(1)}, u32[]{:S(2)}, u32[]{:S(2)}) collective-permute-start(bf16[128,512]{1,0:T(8,128)(2,1)S(1)} %pad_maximum_fusion.9), channel_id=1, source_target_pairs={{0,128},{64,192},{128,0},{192,64},{1,129},{65,193},{129,1},{193,65... | collective-permute-start | bytes 393224 | tf_op jit(solution)/shard_map/ppermute | solution.py:20
  25.6 18.4 %collective-permute-start.7 = (bf16[128,512]{1,0:T(8,128)(2,1)S(1)}, bf16[128,512]{1,0:T(8,128)(2,1)S(1)}, u32[]{:S(2)}, u32[]{:S(2)}) collective-permute-start(bf16[128,512]{1,0:T(8,128)(2,1)S(1)} %pad_maximum_fusion.9), channel_id=1, source_target_pairs={{0,64},{64,128},{128,192},{192,0},{1,65},{65,129},{129,193},{193,1... | collective-permute-start | bytes 393224 | tf_op jit(solution)/shard_map/ppermute | solution.py:20
  26.7 11.1 %collective-permute-start.6 = (f32[128,8]{0,1:T(8,128)S(1)}, f32[128,8]{0,1:T(8,128)S(1)}, u32[]{:S(2)}, u32[]{:S(2)}) collective-permute-start(f32[128,8]{0,1:T(8,128)S(1)} %add.342), channel_id=1, source_target_pairs={{0,128},{64,192},{128,0},{192,64},{1,129},{65,193},{129,1},{193,65... | collective-permute-start | bytes 12296 | tf_op jit(solution)/shard_map/ppermute | solution.py:29
  28.1 11.8 %collective-permute-start.12 = (bf16[32,512]{1,0:T(8,128)(2,1)S(1)}, bf16[32,512]{1,0:T(8,128)(2,1)S(1)}, u32[]{:S(2)}, u32[]{:S(2)}) collective-permute-start(bf16[32,512]{1,0:T(8,128)(2,1)S(1)} %get-tuple-element.208), channel_id=1, source_target_pairs={{0,24},{8,0},{16,8},{24,16},{1,25},{9,1},{17,9},{25,17},{2,26},{10... | collective-permute-start | bytes 98312 | tf_op jit(solution)/shard_map/ppermute | solution.py:20
  37.8 5.4 %collective-permute-start.11 = (bf16[32,512]{1,0:T(8,128)(2,1)S(1)}, bf16[32,512]{1,0:T(8,128)(2,1)S(1)}, u32[]{:S(2)}, u32[]{:S(2)}) collective-permute-start(bf16[32,512]{1,0:T(8,128)(2,1)S(1)} %get-tuple-element.209), channel_id=1, source_target_pairs={{0,16},{8,24},{16,0},{24,8},{1,17},{9,25},{17,1},{25,9},{2,18},{10... | collective-permute-start | bytes 98312 | tf_op jit(solution)/shard_map/ppermute | solution.py:20
  44.1 24.8 %collective-permute-start.20 = (bf16[3,224,2048]{2,1,0:T(8,128)(2,1)}, bf16[3,224,2048]{2,1,0:T(8,128)(2,1)S(1)}, u32[]{:S(2)}, u32[]{:S(2)}) collective-permute-start(bf16[3,224,2048]{2,1,0:T(8,128)(2,1)} %get-tuple-element.105), channel_id=1, source_target_pairs={{0,32},{32,0},{1,33},{33,1},{2,34},{34,2},{3,35},{35,3},{4,36},{36... | collective-permute-start | bytes 8257544 | tf_op jit(solution)/shard_map/ppermute | solution.py:24
  44.3 17.0 %collective-permute-start.15 = (bf16[128,512]{1,0:T(8,128)(2,1)S(1)}, bf16[128,512]{1,0:T(8,128)(2,1)S(1)}, u32[]{:S(2)}, u32[]{:S(2)}) collective-permute-start(bf16[128,512]{1,0:T(8,128)(2,1)S(1)} %pad_maximum_fusion.10), channel_id=1, source_target_pairs={{0,192},{64,0},{128,64},{192,128},{1,193},{65,1},{129,65},{193,129... | collective-permute-start | bytes 393224 | tf_op jit(solution)/shard_map/ppermute | solution.py:20
  47.6 15.4 %collective-permute-start.14 = (bf16[128,512]{1,0:T(8,128)(2,1)S(1)}, bf16[128,512]{1,0:T(8,128)(2,1)S(1)}, u32[]{:S(2)}, u32[]{:S(2)}) collective-permute-start(bf16[128,512]{1,0:T(8,128)(2,1)S(1)} %pad_maximum_fusion.10), channel_id=1, source_target_pairs={{0,128},{64,192},{128,0},{192,64},{1,129},{65,193},{129,1},{193,65... | collective-permute-start | bytes 393224 | tf_op jit(solution)/shard_map/ppermute | solution.py:20
  47.6 6.8 %collective-permute-start.18 = (bf16[2,32,640]{2,1,0:T(8,128)(2,1)S(1)}, bf16[2,32,640]{2,1,0:T(8,128)(2,1)S(1)}, u32[]{:S(2)}, u32[]{:S(2)}) collective-permute-start(bf16[2,32,640]{2,1,0:T(8,128)(2,1)S(1)} %get-tuple-element.197), channel_id=1, source_target_pairs={{0,24},{8,0},{16,8},{24,16},{1,25},{9,1},{17,9},{25,17},{2,26},{10... | collective-permute-start | bytes 245768 | tf_op jit(solution)/shard_map/ppermute | solution.py:20
  47.9 7.5 %collective-permute-start.17 = (bf16[2,32,640]{2,1,0:T(8,128)(2,1)S(1)}, bf16[2,32,640]{2,1,0:T(8,128)(2,1)S(1)}, u32[]{:S(2)}, u32[]{:S(2)}) collective-permute-start(bf16[2,32,640]{2,1,0:T(8,128)(2,1)S(1)} %get-tuple-element.196), channel_id=1, source_target_pairs={{0,16},{8,24},{16,0},{24,8},{1,17},{9,25},{17,1},{25,9},{2,18},{10... | collective-permute-start | bytes 245768 | tf_op jit(solution)/shard_map/ppermute | solution.py:20
  54.4 13.2 %collective-permute-start.19 = (bf16[2,224,1024]{2,1,0:T(8,128)(2,1)S(1)}, bf16[2,224,1024]{2,1,0:T(8,128)(2,1)S(1)}, u32[]{:S(2)}, u32[]{:S(2)}) collective-permute-start(bf16[2,224,1024]{2,1,0:T(8,128)(2,1)S(1)} %pad_maximum_fusion.1), channel_id=1, source_target_pairs={{0,32},{32,0},{1,33},{33,1},{2,34},{34,2},{3,35},{35,3},{4,36},{36... | collective-permute-start | bytes 2752520 | tf_op jit(solution)/shard_map/ppermute | solution.py:24
  59.9 6.8 %collective-permute-start.13 = (bf16[128,512]{1,0:T(8,128)(2,1)S(1)}, bf16[128,512]{1,0:T(8,128)(2,1)S(1)}, u32[]{:S(2)}, u32[]{:S(2)}) collective-permute-start(bf16[128,512]{1,0:T(8,128)(2,1)S(1)} %pad_maximum_fusion.10), channel_id=1, source_target_pairs={{0,64},{64,128},{128,192},{192,0},{1,65},{65,129},{129,193},{193,1... | collective-permute-start | bytes 393224 | tf_op jit(solution)/shard_map/ppermute | solution.py:20
  61.3 16.2 %collective-permute-start.21 = (bf16[128,2048]{1,0:T(8,128)(2,1)S(1)}, bf16[128,2048]{1,0:T(8,128)(2,1)}, u32[]{:S(2)}, u32[]{:S(2)}) collective-permute-start(bf16[128,2048]{1,0:T(8,128)(2,1)S(1)} %pad_maximum_fusion.2.refs_0_), channel_id=1, source_target_pairs={{0,1},{1,2},{2,3},{3,0},{4,5},{5,6},{6,7},{7,4},{8,9},{9,10},{10,1... | collective-permute-start | bytes 1572872 | tf_op jit(solution)/shard_map/ppermute | solution.py:20
  62.9 16.6 %collective-permute-start.22 = (bf16[128,2048]{1,0:T(8,128)(2,1)S(1)}, bf16[128,2048]{1,0:T(8,128)(2,1)}, u32[]{:S(2)}, u32[]{:S(2)}) collective-permute-start(bf16[128,2048]{1,0:T(8,128)(2,1)S(1)} %pad_maximum_fusion.2.refs_0_), channel_id=1, source_target_pairs={{0,3},{1,0},{2,1},{3,2},{4,7},{5,4},{6,5},{7,6},{8,11},{9,8},{10,9... | collective-permute-start | bytes 1572872 | tf_op jit(solution)/shard_map/ppermute | solution.py:20
  69.0 21.4 %collective-permute-start.24 = (bf16[128,2048]{1,0:T(8,128)(2,1)}, bf16[128,2048]{1,0:T(8,128)(2,1)}, u32[]{:S(2)}, u32[]{:S(2)}) collective-permute-start(bf16[128,2048]{1,0:T(8,128)(2,1)} %pad_maximum_fusion.3.refs_1_), channel_id=1, source_target_pairs={{0,1},{1,2},{2,3},{3,0},{4,5},{5,6},{6,7},{7,4},{8,9},{9,10},{10,1... | collective-permute-start | bytes 1572872 | tf_op jit(solution)/shard_map/ppermute | solution.py:20
  70.5 19.8 %collective-permute-start.25 = (bf16[128,2048]{1,0:T(8,128)(2,1)}, bf16[128,2048]{1,0:T(8,128)(2,1)}, u32[]{:S(2)}, u32[]{:S(2)}) collective-permute-start(bf16[128,2048]{1,0:T(8,128)(2,1)} %pad_maximum_fusion.3.refs_1_), channel_id=1, source_target_pairs={{0,3},{1,0},{2,1},{3,2},{4,7},{5,4},{6,5},{7,6},{8,11},{9,8},{10,9... | collective-permute-start | bytes 1572872 | tf_op jit(solution)/shard_map/ppermute | solution.py:20
  73.1 35.1 %collective-permute-start.31 = (bf16[128,512]{1,0:T(8,128)(2,1)S(1)}, bf16[128,512]{1,0:T(8,128)(2,1)}, u32[]{:S(2)}, u32[]{:S(2)}) collective-permute-start(bf16[128,512]{1,0:T(8,128)(2,1)S(1)} %slice.237), channel_id=1, source_target_pairs={{0,192},{64,0},{128,64},{192,128},{1,193},{65,1},{129,65},{193,129... | collective-permute-start | bytes 393224 | tf_op jit(solution)/shard_map/ppermute | solution.py:20
  77.5 31.0 %collective-permute-start.30 = (bf16[128,512]{1,0:T(8,128)(2,1)S(1)}, bf16[128,512]{1,0:T(8,128)(2,1)}, u32[]{:S(2)}, u32[]{:S(2)}) collective-permute-start(bf16[128,512]{1,0:T(8,128)(2,1)S(1)} %slice.237), channel_id=1, source_target_pairs={{0,128},{64,192},{128,0},{192,64},{1,129},{65,193},{129,1},{193,65... | collective-permute-start | bytes 393224 | tf_op jit(solution)/shard_map/ppermute | solution.py:20
  79.5 10.8 %collective-permute-start.23 = (bf16[128,640]{1,0:T(8,128)(2,1)}, bf16[128,640]{1,0:T(8,128)(2,1)S(1)}, u32[]{:S(2)}, u32[]{:S(2)}) collective-permute-start(bf16[128,640]{1,0:T(8,128)(2,1)} %get-tuple-element.107), channel_id=1, source_target_pairs={{0,4},{4,0},{1,5},{5,1},{2,6},{6,2},{3,7},{7,3},{8,12},{12,8},{9,1... | collective-permute-start | bytes 491528 | tf_op jit(solution)/shard_map/ppermute | solution.py:24
  95.2 36.7 %collective-permute-start.26 = (f32[2,768,256]{2,1,0:T(8,128)}, f32[2,768,256]{2,1,0:T(8,128)}, u32[]{:S(2)}, u32[]{:S(2)}) collective-permute-start(f32[2,768,256]{2,1,0:T(8,128)} %pull.2.refs_0_), channel_id=1, source_target_pairs={{0,32},{32,0},{1,33},{33,1},{2,34},{34,2},{3,35},{35,3},{4,36},{36... | collective-permute-start | bytes 4718600 | tf_op jit(solution)/shard_map/ppermute | solution.py:24
  95.3 16.2 %collective-permute-start.29 = (bf16[128,512]{1,0:T(8,128)(2,1)S(1)}, bf16[128,512]{1,0:T(8,128)(2,1)S(1)}, u32[]{:S(2)}, u32[]{:S(2)}) collective-permute-start(bf16[128,512]{1,0:T(8,128)(2,1)S(1)} %slice.237), channel_id=1, source_target_pairs={{0,64},{64,128},{128,192},{192,0},{1,65},{65,129},{129,193},{193,1... | collective-permute-start | bytes 393224 | tf_op jit(solution)/shard_map/ppermute | solution.py:20
  97.9 14.6 %collective-permute-start.34 = (bf16[128,512]{1,0:T(8,128)(2,1)S(1)}, bf16[128,512]{1,0:T(8,128)(2,1)S(1)}, u32[]{:S(2)}, u32[]{:S(2)}) collective-permute-start(bf16[128,512]{1,0:T(8,128)(2,1)S(1)} %slice.238), channel_id=1, source_target_pairs={{0,192},{64,0},{128,64},{192,128},{1,193},{65,1},{129,65},{193,129... | collective-permute-start | bytes 393224 | tf_op jit(solution)/shard_map/ppermute | solution.py:20
  108.2 15.1 %collective-permute-start.27 = (bf16[128,2048]{1,0:T(8,128)(2,1)}, bf16[128,2048]{1,0:T(8,128)(2,1)S(1)}, u32[]{:S(2)}, u32[]{:S(2)}) collective-permute-start(bf16[128,2048]{1,0:T(8,128)(2,1)} %collective-permute-done.21.refs_4_), channel_id=1, source_target_pairs={{0,1},{1,2},{2,3},{3,0},{4,5},{5,6},{6,7},{7,4},{8,9},{9,10},{10,1... | collective-permute-start | bytes 1572872 | tf_op jit(solution)/shard_map/ppermute | solution.py:20
  108.5 14.8 %collective-permute-start.28 = (bf16[128,2048]{1,0:T(8,128)(2,1)}, bf16[128,2048]{1,0:T(8,128)(2,1)}, u32[]{:S(2)}, u32[]{:S(2)}) collective-permute-start(bf16[128,2048]{1,0:T(8,128)(2,1)} %collective-permute-done.25.refs_3_), channel_id=1, source_target_pairs={{0,3},{1,0},{2,1},{3,2},{4,7},{5,4},{6,5},{7,6},{8,11},{9,8},{10,9... | collective-permute-start | bytes 1572872 | tf_op jit(solution)/shard_map/ppermute | solution.py:20
  111.4 11.2 %collective-permute-start.33 = (bf16[128,512]{1,0:T(8,128)(2,1)S(1)}, bf16[128,512]{1,0:T(8,128)(2,1)S(1)}, u32[]{:S(2)}, u32[]{:S(2)}) collective-permute-start(bf16[128,512]{1,0:T(8,128)(2,1)S(1)} %slice.238), channel_id=1, source_target_pairs={{0,128},{64,192},{128,0},{192,64},{1,129},{65,193},{129,1},{193,65... | collective-permute-start | bytes 393224 | tf_op jit(solution)/shard_map/ppermute | solution.py:20
  112.5 10.1 %collective-permute-start.32 = (bf16[128,512]{1,0:T(8,128)(2,1)S(1)}, bf16[128,512]{1,0:T(8,128)(2,1)S(1)}, u32[]{:S(2)}, u32[]{:S(2)}) collective-permute-start(bf16[128,512]{1,0:T(8,128)(2,1)S(1)} %slice.238), channel_id=1, source_target_pairs={{0,64},{64,128},{128,192},{192,0},{1,65},{65,129},{129,193},{193,1... | collective-permute-start | bytes 393224 | tf_op jit(solution)/shard_map/ppermute | solution.py:20
  123.4 28.8 %collective-permute-start.38 = (bf16[256,2176]{1,0:T(8,128)(2,1)S(1)}, bf16[256,2176]{1,0:T(8,128)(2,1)S(1)}, u32[]{:S(2)}, u32[]{:S(2)}) collective-permute-start(bf16[256,2176]{1,0:T(8,128)(2,1)S(1)} %maximum_maximum_fusion.refs_0_.refs_8_), channel_id=1, source_target_pairs={{0,1},{1,2},{2,3},{3,0},{4,5},{5,6},{6,7},{7,4},{8,9},{9,10},{10,1... | collective-permute-start | bytes 3342344 | tf_op jit(solution)/shard_map/ppermute | solution.py:20
  123.9 28.3 %collective-permute-start.39 = (bf16[256,2176]{1,0:T(8,128)(2,1)S(1)}, bf16[256,2176]{1,0:T(8,128)(2,1)S(1)}, u32[]{:S(2)}, u32[]{:S(2)}) collective-permute-start(bf16[256,2176]{1,0:T(8,128)(2,1)S(1)} %maximum_maximum_fusion.refs_0_.refs_8_), channel_id=1, source_target_pairs={{0,3},{1,0},{2,1},{3,2},{4,7},{5,4},{6,5},{7,6},{8,11},{9,8},{10,9... | collective-permute-start | bytes 3342344 | tf_op jit(solution)/shard_map/ppermute | solution.py:20
  144.3 19.2 %collective-permute-start.36 = (bf16[128,2048]{1,0:T(8,128)(2,1)}, bf16[128,2048]{1,0:T(8,128)(2,1)S(1)}, u32[]{:S(2)}, u32[]{:S(2)}) collective-permute-start(bf16[128,2048]{1,0:T(8,128)(2,1)} %get-tuple-element.122), channel_id=1, source_target_pairs={{0,1},{1,2},{2,3},{3,0},{4,5},{5,6},{6,7},{7,4},{8,9},{9,10},{10,1... | collective-permute-start | bytes 1572872 | tf_op jit(solution)/shard_map/ppermute | solution.py:20
  144.3 20.0 %collective-permute-start.37 = (bf16[128,2048]{1,0:T(8,128)(2,1)}, bf16[128,2048]{1,0:T(8,128)(2,1)S(1)}, u32[]{:S(2)}, u32[]{:S(2)}) collective-permute-start(bf16[128,2048]{1,0:T(8,128)(2,1)} %get-tuple-element.123), channel_id=1, source_target_pairs={{0,3},{1,0},{2,1},{3,2},{4,7},{5,4},{6,5},{7,6},{8,11},{9,8},{10,9... | collective-permute-start | bytes 1572872 | tf_op jit(solution)/shard_map/ppermute | solution.py:20
  147.6 34.2 %collective-permute-start.42 = (bf16[128,2048]{1,0:T(8,128)(2,1)}, bf16[128,2048]{1,0:T(8,128)(2,1)}, u32[]{:S(2)}, u32[]{:S(2)}) collective-permute-start(bf16[128,2048]{1,0:T(8,128)(2,1)} %get-tuple-element.130), channel_id=1, source_target_pairs={{0,1},{1,2},{2,3},{3,0},{4,5},{5,6},{6,7},{7,4},{8,9},{9,10},{10,1... | collective-permute-start | bytes 1572872 | tf_op jit(solution)/shard_map/ppermute | solution.py:20
  152.2 20.8 %collective-permute-start.44 = (f32[256]{0:T(256)S(1)}, f32[256]{0:T(256)S(1)}, u32[]{:S(2)}, u32[]{:S(2)}) collective-permute-start(f32[256]{0:T(256)S(1)} %get-tuple-element.180), channel_id=1, source_target_pairs={{0,1},{1,2},{2,3},{3,0},{4,5},{5,6},{6,7},{7,4},{8,9},{9,10},{10,1... | collective-permute-start | bytes 3080 | tf_op jit(solution)/shard_map/ppermute | solution.py:20
  152.2 20.8 %collective-permute-start.45 = (f32[256]{0:T(256)S(1)}, f32[256]{0:T(256)S(1)}, u32[]{:S(2)}, u32[]{:S(2)}) collective-permute-start(f32[256]{0:T(256)S(1)} %get-tuple-element.179), channel_id=1, source_target_pairs={{0,3},{1,0},{2,1},{3,2},{4,7},{5,4},{6,5},{7,6},{8,11},{9,8},{10,9... | collective-permute-start | bytes 3080 | tf_op jit(solution)/shard_map/ppermute | solution.py:20
  163.4 10.2 %collective-permute-start.46 = (f32[256]{0:T(256)S(1)}, f32[256]{0:T(256)S(1)}, u32[]{:S(2)}, u32[]{:S(2)}) collective-permute-start(f32[256]{0:T(256)S(1)} %get-tuple-element.178), channel_id=1, source_target_pairs={{0,2},{1,3},{2,0},{3,1},{4,6},{5,7},{6,4},{7,5},{8,10},{9,11},{10,... | collective-permute-start | bytes 3080 | tf_op jit(solution)/shard_map/ppermute | solution.py:20
  165.6 16.3 %collective-permute-start.43 = (bf16[128,2048]{1,0:T(8,128)(2,1)S(1)}, bf16[128,2048]{1,0:T(8,128)(2,1)}, u32[]{:S(2)}, u32[]{:S(2)}) collective-permute-start(bf16[128,2048]{1,0:T(8,128)(2,1)S(1)} %add_convert_fusion.1), channel_id=1, source_target_pairs={{0,3},{1,0},{2,1},{3,2},{4,7},{5,4},{6,5},{7,6},{8,11},{9,8},{10,9... | collective-permute-start | bytes 1572872 | tf_op jit(solution)/shard_map/ppermute | solution.py:20
  178.1 14.6 %collective-permute-start.41 = (bf16[128,2048]{1,0:T(8,128)(2,1)}, bf16[128,2048]{1,0:T(8,128)(2,1)S(1)}, u32[]{:S(2)}, u32[]{:S(2)}) collective-permute-start(bf16[128,2048]{1,0:T(8,128)(2,1)} %get-tuple-element.128), channel_id=1, source_target_pairs={{0,3},{1,0},{2,1},{3,2},{4,7},{5,4},{6,5},{7,6},{8,11},{9,8},{10,9... | collective-permute-start | bytes 1572872 | tf_op jit(solution)/shard_map/ppermute | solution.py:20
  178.8 13.9 %collective-permute-start.40 = (bf16[128,2048]{1,0:T(8,128)(2,1)}, bf16[128,2048]{1,0:T(8,128)(2,1)}, u32[]{:S(2)}, u32[]{:S(2)}) collective-permute-start(bf16[128,2048]{1,0:T(8,128)(2,1)} %add_convert_fusion.3), channel_id=1, source_target_pairs={{0,1},{1,2},{2,3},{3,0},{4,5},{5,6},{6,7},{7,4},{8,9},{9,10},{10,1... | collective-permute-start | bytes 1572872 | tf_op jit(solution)/shard_map/ppermute | solution.py:20
  181.8 7.8 %collective-permute-start.54 = (f32[4,32]{1,0:T(4,128)S(1)}, f32[4,32]{1,0:T(4,128)S(1)}, u32[]{:S(2)}, u32[]{:S(2)}) collective-permute-start(f32[4,32]{1,0:T(4,128)S(1)} %get-tuple-element.230), channel_id=1, source_target_pairs={{0,4},{4,0},{1,5},{5,1},{2,6},{6,2},{3,7},{7,3},{8,12},{12,8},{9,1... | collective-permute-start | bytes 1544 | tf_op jit(solution)/shard_map/ppermute | solution.py:24
  187.0 15.4 %collective-permute-start.49 = (bf16[128,512]{1,0:T(8,128)(2,1)}, bf16[128,512]{1,0:T(8,128)(2,1)S(1)}, u32[]{:S(2)}, u32[]{:S(2)}) collective-permute-start(bf16[128,512]{1,0:T(8,128)(2,1)} %get-tuple-element.192), channel_id=1, source_target_pairs={{0,192},{64,0},{128,64},{192,128},{1,193},{65,1},{129,65},{193,129... | collective-permute-start | bytes 393224 | tf_op jit(solution)/shard_map/ppermute | solution.py:20
  188.1 14.3 %collective-permute-start.50 = (bf16[128,512]{1,0:T(8,128)(2,1)}, bf16[128,512]{1,0:T(8,128)(2,1)}, u32[]{:S(2)}, u32[]{:S(2)}) collective-permute-start(bf16[128,512]{1,0:T(8,128)(2,1)} %get-tuple-element.191), channel_id=1, source_target_pairs={{0,128},{64,192},{128,0},{192,64},{1,129},{65,193},{129,1},{193,65... | collective-permute-start | bytes 393224 | tf_op jit(solution)/shard_map/ppermute | solution.py:20
  194.0 8.4 %collective-permute-start.51 = (bf16[128,512]{1,0:T(8,128)(2,1)}, bf16[128,512]{1,0:T(8,128)(2,1)}, u32[]{:S(2)}, u32[]{:S(2)}) collective-permute-start(bf16[128,512]{1,0:T(8,128)(2,1)} %get-tuple-element.190), channel_id=1, source_target_pairs={{0,64},{64,128},{128,192},{192,0},{1,65},{65,129},{129,193},{193,1... | collective-permute-start | bytes 393224 | tf_op jit(solution)/shard_map/ppermute | solution.py:20
  197.8 11.0 %collective-permute-start.52 = (bf16[128,2176]{1,0:T(8,128)(2,1)}, bf16[128,2176]{1,0:T(8,128)(2,1)S(1)}, u32[]{:S(2)}, u32[]{:S(2)}) collective-permute-start(bf16[128,2176]{1,0:T(8,128)(2,1)} %slice.248), channel_id=1, source_target_pairs={{0,1},{1,2},{2,3},{3,0},{4,5},{5,6},{6,7},{7,4},{8,9},{9,10},{10,1... | collective-permute-start | bytes 1671176 | tf_op jit(solution)/shard_map/ppermute | solution.py:20
  197.8 11.0 %collective-permute-start.53 = (bf16[128,2176]{1,0:T(8,128)(2,1)S(1)}, bf16[128,2176]{1,0:T(8,128)(2,1)S(1)}, u32[]{:S(2)}, u32[]{:S(2)}) collective-permute-start(bf16[128,2176]{1,0:T(8,128)(2,1)S(1)} %slice.249), channel_id=1, source_target_pairs={{0,3},{1,0},{2,1},{3,2},{4,7},{5,4},{6,5},{7,6},{8,11},{9,8},{10,9... | collective-permute-start | bytes 1671176 | tf_op jit(solution)/shard_map/ppermute | solution.py:20
  210.2 35.4 %collective-permute-start.61 = (bf16[128,512]{1,0:T(8,128)(2,1)S(1)}, bf16[128,512]{1,0:T(8,128)(2,1)S(1)}, u32[]{:S(2)}, u32[]{:S(2)}) collective-permute-start(bf16[128,512]{1,0:T(8,128)(2,1)S(1)} %add_convert_fusion.4), channel_id=1, source_target_pairs={{0,4},{4,0},{1,5},{5,1},{2,6},{6,2},{3,7},{7,3},{8,12},{12,8},{9,1... | collective-permute-start | bytes 393224 | tf_op jit(solution)/shard_map/ppermute | solution.py:24
  222.6 12.8 %collective-permute-start.58 = (bf16[128,512]{1,0:T(8,128)(2,1)S(1)}, bf16[128,512]{1,0:T(8,128)(2,1)S(1)}, u32[]{:S(2)}, u32[]{:S(2)}) collective-permute-start(bf16[128,512]{1,0:T(8,128)(2,1)S(1)} %get-tuple-element.189), channel_id=1, source_target_pairs={{0,192},{64,0},{128,64},{192,128},{1,193},{65,1},{129,65},{193,129... | collective-permute-start | bytes 393224 | tf_op jit(solution)/shard_map/ppermute | solution.py:20
  225.5 9.9 %collective-permute-start.59 = (bf16[128,512]{1,0:T(8,128)(2,1)S(1)}, bf16[128,512]{1,0:T(8,128)(2,1)S(1)}, u32[]{:S(2)}, u32[]{:S(2)}) collective-permute-start(bf16[128,512]{1,0:T(8,128)(2,1)S(1)} %get-tuple-element.188), channel_id=1, source_target_pairs={{0,128},{64,192},{128,0},{192,64},{1,129},{65,193},{129,1},{193,65... | collective-permute-start | bytes 393224 | tf_op jit(solution)/shard_map/ppermute | solution.py:20
  225.5 9.9 %collective-permute-start.60 = (bf16[128,512]{1,0:T(8,128)(2,1)S(1)}, bf16[128,512]{1,0:T(8,128)(2,1)S(1)}, u32[]{:S(2)}, u32[]{:S(2)}) collective-permute-start(bf16[128,512]{1,0:T(8,128)(2,1)S(1)} %get-tuple-element.187), channel_id=1, source_target_pairs={{0,64},{64,128},{128,192},{192,0},{1,65},{65,129},{129,193},{193,1... | collective-permute-start | bytes 393224 | tf_op jit(solution)/shard_map/ppermute | solution.py:20
  240.1 5.4 %collective-permute-start.62 = (f32[16,512]{1,0:T(8,128)S(1)}, f32[16,512]{1,0:T(8,128)S(1)}, u32[]{:S(2)}, u32[]{:S(2)}) collective-permute-start(f32[16,512]{1,0:T(8,128)S(1)} %concatenate.71), channel_id=1, source_target_pairs={{0,2},{1,3},{2,0},{3,1},{4,6},{5,7},{6,4},{7,5},{8,10},{9,11},{10,... | collective-permute-start | bytes 98312 | tf_op jit(solution)/shard_map/ppermute | solution.py:20
  245.5 7.0 %collective-permute-start.69 = (f32[16,512]{1,0:T(8,128)S(1)}, f32[16,512]{1,0:T(8,128)S(1)}, u32[]{:S(2)}, u32[]{:S(2)}) collective-permute-start(f32[16,512]{1,0:T(8,128)S(1)} %add_add_fusion.1), channel_id=1, source_target_pairs={{0,8},{8,16},{16,24},{24,0},{1,9},{9,17},{17,25},{25,1},{2,10},{10... | collective-permute-start | bytes 98312 | tf_op jit(solution)/shard_map/ppermute | solution.py:20
  246.2 6.5 %collective-permute-start.70 = (f32[16,512]{1,0:T(8,128)S(1)}, f32[16,512]{1,0:T(8,128)S(1)}, u32[]{:S(2)}, u32[]{:S(2)}) collective-permute-start(f32[16,512]{1,0:T(8,128)S(1)} %add_add_fusion.1), channel_id=1, source_target_pairs={{0,24},{8,0},{16,8},{24,16},{1,25},{9,1},{17,9},{25,17},{2,26},{10... | collective-permute-start | bytes 98312 | tf_op jit(solution)/shard_map/ppermute | solution.py:20
  247.6 5.4 %collective-permute-start.68 = (f32[16,512]{1,0:T(8,128)S(1)}, f32[16,512]{1,0:T(8,128)S(1)}, u32[]{:S(2)}, u32[]{:S(2)}) collective-permute-start(f32[16,512]{1,0:T(8,128)S(1)} %add_add_fusion.1), channel_id=1, source_target_pairs={{0,16},{8,24},{16,0},{24,8},{1,17},{9,25},{17,1},{25,9},{2,18},{10... | collective-permute-start | bytes 98312 | tf_op jit(solution)/shard_map/ppermute | solution.py:20
  250.5 5.8 %collective-permute-start.66 = (bf16[2,32,512]{2,1,0:T(8,128)(2,1)S(1)}, bf16[2,32,512]{2,1,0:T(8,128)(2,1)S(1)}, u32[]{:S(2)}, u32[]{:S(2)}) collective-permute-start(bf16[2,32,512]{2,1,0:T(8,128)(2,1)S(1)} %get-tuple-element.201), channel_id=1, source_target_pairs={{0,16},{8,24},{16,0},{24,8},{1,17},{9,25},{17,1},{25,9},{2,18},{10... | collective-permute-start | bytes 196616 | tf_op jit(solution)/shard_map/ppermute | solution.py:20
  252.5 5.5 %collective-permute-start.65 = (bf16[2,32,512]{2,1,0:T(8,128)(2,1)S(1)}, bf16[2,32,512]{2,1,0:T(8,128)(2,1)S(1)}, u32[]{:S(2)}, u32[]{:S(2)}) collective-permute-start(bf16[2,32,512]{2,1,0:T(8,128)(2,1)S(1)} %get-tuple-element.200), channel_id=1, source_target_pairs={{0,24},{8,0},{16,8},{24,16},{1,25},{9,1},{17,9},{25,17},{2,26},{10... | collective-permute-start | bytes 196616 | tf_op jit(solution)/shard_map/ppermute | solution.py:20
  258.1 7.9 %collective-permute-start.71 = (f32[16,512]{1,0:T(8,128)S(1)}, f32[16,512]{1,0:T(8,128)S(1)}, u32[]{:S(2)}, u32[]{:S(2)}) collective-permute-start(f32[16,512]{1,0:T(8,128)S(1)} %add_add_fusion), channel_id=1, source_target_pairs={{0,4},{4,0},{1,5},{5,1},{2,6},{6,2},{3,7},{7,3},{8,12},{12,8},{9,1... | collective-permute-start | bytes 98312 | tf_op jit(solution)/shard_map/ppermute | solution.py:24
  268.5 13.2 %collective-permute-start.76 = (bf16[224,2048]{1,0:T(8,128)(2,1)}, bf16[224,2048]{1,0:T(8,128)(2,1)S(1)}, u32[]{:S(2)}, u32[]{:S(2)}) collective-permute-start(bf16[224,2048]{1,0:T(8,128)(2,1)} %get-tuple-element.169), channel_id=1, source_target_pairs={{0,32},{32,0},{1,33},{33,1},{2,34},{34,2},{3,35},{35,3},{4,36},{36... | collective-permute-start | bytes 2752520 | tf_op jit(solution)/shard_map/ppermute | solution.py:24
  269.0 12.7 %collective-permute-start.77 = (bf16[224,2048]{1,0:T(8,128)(2,1)S(1)}, bf16[224,2048]{1,0:T(8,128)(2,1)S(1)}, u32[]{:S(2)}, u32[]{:S(2)}) collective-permute-start(bf16[224,2048]{1,0:T(8,128)(2,1)S(1)} %copy-done.30), channel_id=1, source_target_pairs={{0,32},{32,0},{1,33},{33,1},{2,34},{34,2},{3,35},{35,3},{4,36},{36... | collective-permute-start | bytes 2752520 | tf_op jit(solution)/shard_map/ppermute | solution.py:24
  269.1 12.6 %collective-permute-start.78 = (bf16[224,2048]{1,0:T(8,128)(2,1)}, bf16[224,2048]{1,0:T(8,128)(2,1)S(1)}, u32[]{:S(2)}, u32[]{:S(2)}) collective-permute-start(bf16[224,2048]{1,0:T(8,128)(2,1)} %get-tuple-element.173), channel_id=1, source_target_pairs={{0,32},{32,0},{1,33},{33,1},{2,34},{34,2},{3,35},{35,3},{4,36},{36... | collective-permute-start | bytes 2752520 | tf_op jit(solution)/shard_map/ppermute | solution.py:24
  269.7 5.6 %collective-permute-start.74 = (f32[8,128]{1,0:T(8,128)S(1)}, f32[8,128]{1,0:T(8,128)S(1)}, u32[]{:S(2)}, u32[]{:S(2)}) collective-permute-start(f32[8,128]{1,0:T(8,128)S(1)} %broadcast_add_fusion), channel_id=1, source_target_pairs={{0,64},{64,128},{128,192},{192,0},{1,65},{65,129},{129,193},{193,1... | collective-permute-start | bytes 12296 | tf_op jit(solution)/shard_map/ppermute | solution.py:20
  (48 other events, 664.9 us)
where the time goes:
time: 295 us; the launch traced here: 290 us
  starting transfers between devices  114 us (39%)
  waiting for transfers between devices  87.1 us (30%)
  Pallas kernels  52.8 us (18%)
  other arithmetic  18.1 us (6%)
  local copies, waits for them, and re-layouts  9.07 us (3%)
  between operations  5.11 us (2%)
  matrix products  4.05 us (1%)
    ppermute x61, starting transfers between devices, turn(): lax.ppermute(value, axis, [(i, (i + step) % RING) for i in range(RING)])  90.4 us
    ppermute x61, waiting for transfers between devices, turn(): lax.ppermute(value, axis, [(i, (i + step) % RING) for i in range(RING)])  64.5 us
    ppermute x14, starting transfers between devices, swap(): return lax.ppermute(value, axis, [(0, 1), (1, 0)])  19.1 us
    pallas_call x2, Pallas kernels, grads_call(): pl.pallas_call(functools.partial(grads_kernel, len(rows), len(lefts), len...  14.6 us
    ppermute x4, waiting for transfers between devices, sum_ring(): lax.ppermute(value, axis, [(i, i ^ bit) for i in range(RING)])  13.9 us
    pallas_call x1, Pallas kernels, slots_call(): pl.pallas_call(functools.partial(slots_kernel, near), grid=(RING,), in_sp...  11.5 us
    ppermute x14, waiting for transfers between devices, swap(): return lax.ppermute(value, axis, [(0, 1), (1, 0)])  8.73 us
    pallas_call x2, Pallas kernels, pull_call(): pl.pallas_call(functools.partial(pull_kernel, len(rows)), grid=(half // s...  8.04 us
  transfers between devices with their start and end apart: 79, of which 33 were waited for; matrix products, arithmetic and copies ran while one was open for 8% of the time, Pallas kernels for 16%

commit v1 on v0

--- a/solution.py
+++ b/solution.py
@@ -274,7 +274,7 @@
 
 def grads_call(rows, gates, lefts, half):
     _, total, hidden_dev = lefts[0].shape
-    step = min(512, half)
+    step = half // RING
     shape = jax.ShapeDtypeStruct
     in_specs = [pl.BlockSpec((r.shape[0], step), lambda j: (0, j)) for r in rows]
     in_specs += [pl.BlockSpec((g.shape[0], LANES), lambda j: (0, half // LANES)) for g in gates]
@@ -291,7 +291,7 @@
         cost_estimate=cost(),
         name="grads",
     )(*rows, *gates, *lefts)
-    return out[0:-1:2], out[1:-1:2], jnp.sum(out[-1])
+    return out[0:-1:2], out[1:-1:2], out[-1]
 
 
 def local(
@@ -461,9 +461,7 @@
     near = add(sums[1][:, :features], *parts[1]).astype(BF16)
 
     far = swap(far, "h")
-    message = jnp.concatenate(
-        [router_term, jnp.full((8, features), down_square + two_square, F32)], axis=0
-    )
+    message = jnp.concatenate([router_term, down_square + two_square], axis=0)
     message = sum_turns(message, "y")
     far, message = barrier((far, message))
     back_dx = exchange_x(jnp.concatenate([near, far], axis=0), -1)
@@ -473,7 +471,8 @@
     other_two = [swap(part, "c") for part in other_two]
     message = sum_pair(message, "h")
     raw_router = message[:experts]
-    square_sum = jnp.full((8, LANES), message[experts, 0] + jnp.sum(raw_router * raw_router), F32)
+    square_sum = jnp.sum(raw_router * raw_router + message[experts:])
+    square_sum = jnp.full((8, LANES), square_sum, F32)
     square_sum = sum_turns(sum_pair(square_sum, "c"), "z")[0, 0]
     row_count = features // (8 * RING)
     raw_router = lax.dynamic_slice_in_dim(

time: 295 us -> 292 us (0.990)
  no operation moved by 1% of the time
where the time goes in v1:
time: 292 us; the launch traced here: 287 us
  starting transfers between devices  114 us (39%)
  waiting for transfers between devices  86.9 us (30%)
  Pallas kernels  52.8 us (18%)
  other arithmetic  17.3 us (6%)
  local copies, waits for them, and re-layouts  9.21 us (3%)
  matrix products  4.05 us (1%)
    ppermute x61, starting transfers between devices, turn(): lax.ppermute(value, axis, [(i, (i + step) % RING) for i in range(RING)])  90.6 us
    ppermute x61, waiting for transfers between devices, turn(): lax.ppermute(value, axis, [(i, (i + step) % RING) for i in range(RING)])  64.4 us
    ppermute x14, starting transfers between devices, swap(): return lax.ppermute(value, axis, [(0, 1), (1, 0)])  19.2 us
    pallas_call x2, Pallas kernels, grads_call(): pl.pallas_call(functools.partial(grads_kernel, len(rows), len(lefts), len...  14.6 us
    ppermute x4, waiting for transfers between devices, sum_ring(): lax.ppermute(value, axis, [(i, i ^ bit) for i in range(RING)])  13.9 us
    pallas_call x1, Pallas kernels, slots_call(): pl.pallas_call(functools.partial(slots_kernel, near), grid=(RING,), in_sp...  11.5 us
    ppermute x14, waiting for transfers between devices, swap(): return lax.ppermute(value, axis, [(0, 1), (1, 0)])  8.62 us
    pallas_call x2, Pallas kernels, pull_call(): pl.pallas_call(functools.partial(pull_kernel, len(rows)), grid=(half // s...  8.03 us
  transfers between devices with their start and end apart: 79, of which 33 were waited for; matrix products, arithmetic and copies ran while one was open for 8% of the time, Pallas kernels for 16%

profile of v1, /device:TPU:6, one launch (start us, length us, event | category | flops | bytes accessed | tf_op | source)
XLA Modules:
  0.0 286.8 jit_solution(17843582809837211005)
XLA Ops:
  3.4 2.8 collective-permute-start.1
  6.7 7.3 %collective-permute-start.3 = (bf16[128,512]{1,0:T(8,128)(2,1)S(1)}, bf16[128,512]{1,0:T(8,128)(2,1)S(1)}, u32[]{:S(2)}, u32[]{:S(2)}) collective-permute-start(bf16[128,512]{1,0:T(8,128)(2,1)S(1)} %slice.279), channel_id=1, source_target_pairs={{0,4},{4,0},{1,5},{5,1},{2,6},{6,2},{3,7},{7,3},{8,12},{12,8},{9,1... | collective-permute-start | bytes 393224 | tf_op jit(solution)/shard_map/ppermute | solution.py:24
  15.7 6.3 %arrange.1 = (bf16[3,224,2048]{2,1,0:T(8,128)(2,1)}, bf16[3,224,2048]{2,1,0:T(8,128)(2,1)}) custom-call(s32[5]{0:T(128)} %stack.41.place, bf16[224,4096]{1,0:T(8,128)(2,1)} %bitcast.103, bf16[224,4096]{1,0:T(8,128)(2,1)} %bitcast.104, bf16[224,4096]{1,0:T(8,128)(2,1)} %bitcast.105), custom_call_target="tpu_custom_call" | custom-call | flops 1 | bytes 1 | tf_op jit(solution)/shard_map/arrange/pallas_call | solution.py:202
  23.2 1.9 collective-permute-start.9
  26.7 1.5 collective-permute-start.6
  28.3 9.5 %collective-permute-done.6 = f32[128,8]{0,1:T(8,128)S(1)} collective-permute-done((f32[128,8]{0,1:T(8,128)S(1)}, f32[128,8]{0,1:T(8,128)S(1)}, u32[]{:S(2)}, u32[]{:S(2)}) %collective-permute-start.6) | collective-permute-done | bytes 4128 | tf_op jit(solution)/shard_map/ppermute | solution.py:29
  37.8 2.1 collective-permute-start.11
  41.1 2.1 collective-permute-done.11
  44.3 3.2 %collective-permute-start.15 = (bf16[128,512]{1,0:T(8,128)(2,1)S(1)}, bf16[128,512]{1,0:T(8,128)(2,1)S(1)}, u32[]{:S(2)}, u32[]{:S(2)}) collective-permute-start(bf16[128,512]{1,0:T(8,128)(2,1)S(1)} %pad_maximum_fusion.10), channel_id=1, source_target_pairs={{0,192},{64,0},{128,64},{192,128},{1,193},{65,1},{129,65},{193,129... | collective-permute-start | bytes 393224 | tf_op jit(solution)/shard_map/ppermute | solution.py:20
  48.0 3.3 %collective-permute-start.17 = (bf16[2,32,640]{2,1,0:T(8,128)(2,1)S(1)}, bf16[2,32,640]{2,1,0:T(8,128)(2,1)S(1)}, u32[]{:S(2)}, u32[]{:S(2)}) collective-permute-start(bf16[2,32,640]{2,1,0:T(8,128)(2,1)S(1)} %get-tuple-element.196), channel_id=1, source_target_pairs={{0,16},{8,24},{16,0},{24,8},{1,17},{9,25},{17,1},{25,9},{2,18},{10... | collective-permute-start | bytes 245768 | tf_op jit(solution)/shard_map/ppermute | solution.py:20
  51.3 3.1 %collective-permute-done.18 = bf16[2,32,640]{2,1,0:T(8,128)(2,1)S(1)} collective-permute-done((bf16[2,32,640]{2,1,0:T(8,128)(2,1)S(1)}, bf16[2,32,640]{2,1,0:T(8,128)(2,1)S(1)}, u32[]{:S(2)}, u32[]{:S(2)}) %collective-permute-start.18) | collective-permute-done | bytes 81952 | tf_op jit(solution)/shard_map/ppermute | solution.py:20
  55.5 1.7 collective-permute-start.16
  57.2 2.7 collective-permute-done.16
  61.4 1.6 collective-permute-start.21
  62.9 1.7 collective-permute-start.22
  64.6 2.1 collective-permute-done.13
  69.0 1.6 collective-permute-start.24
  70.5 1.7 collective-permute-start.25
  74.3 3.3 %collective-permute-done.21.refs_4_ = bf16[128,2048]{1,0:T(8,128)(2,1)} collective-permute-done((bf16[128,2048]{1,0:T(8,128)(2,1)S(1)}, bf16[128,2048]{1,0:T(8,128)(2,1)}, u32[]{:S(2)}, u32[]{:S(2)}) %collective-permute-start.21) | collective-permute-done | bytes 524320 | tf_op jit(solution)/shard_map/ppermute | solution.py:20
  77.5 2.0 collective-permute-start.30
  79.5 1.4 collective-permute-start.23
  81.0 1.6 fusion.15.source
  82.6 6.0 %sort.1.refs_4_ = bf16[4,1024,224]{2,1,0:T(8,128)(2,1)} custom-call(s32[1024,1]{1,0:T(8,128)} %fusion.15.source, bf16[4,224,1024]{2,1,0:T(8,128)(2,1)} %pad_maximum_fusion.saved), custom_call_target="tpu_custom_call" | custom-call | flops 1 | bytes 1 | tf_op jit(solution)/shard_map/sort/pallas_call | solution.py:99
  88.6 1.7 collective-permute-done.23
  90.3 4.9 %pull.2.refs_0_ = f32[2,768,256]{2,1,0:T(8,128)} custom-call(bf16[128,2048]{1,0:T(8,128)(2,1)} %copy-done.6, bf16[128,2048]{1,0:T(8,128)(2,1)} %pad_maximum_fusion.3.refs_1_, bf16[128,2048]{1,0:T(8,128)(2,1)} %collective-permute-done.22.refs_2_, bf16[128,2048]{1,0:T(8,128)(2,1)} %collective-permute-done.25.refs_3_, ...), custom_call_target="tpu_custom_call" | custom-call | flops 1 | bytes 1 | tf_op jit(solution)/shard_map/pull/pallas_call | solution.py:77
  95.3 2.7 collective-permute-start.29
  98.0 10.2 %collective-permute-start.34 = (bf16[128,512]{1,0:T(8,128)(2,1)S(1)}, bf16[128,512]{1,0:T(8,128)(2,1)S(1)}, u32[]{:S(2)}, u32[]{:S(2)}) collective-permute-start(bf16[128,512]{1,0:T(8,128)(2,1)S(1)} %slice.238), channel_id=1, source_target_pairs={{0,192},{64,0},{128,64},{192,128},{1,193},{65,1},{129,65},{193,129... | collective-permute-start | bytes 393224 | tf_op jit(solution)/shard_map/ppermute | solution.py:20
  108.5 2.9 %collective-permute-start.28 = (bf16[128,2048]{1,0:T(8,128)(2,1)}, bf16[128,2048]{1,0:T(8,128)(2,1)}, u32[]{:S(2)}, u32[]{:S(2)}) collective-permute-start(bf16[128,2048]{1,0:T(8,128)(2,1)} %collective-permute-done.25.refs_3_), channel_id=1, source_target_pairs={{0,3},{1,0},{2,1},{3,2},{4,7},{5,4},{6,5},{7,6},{8,11},{9,8},{10,9... | collective-permute-start | bytes 1572872 | tf_op jit(solution)/shard_map/ppermute | solution.py:20
  114.6 8.1 %collective-permute-done.33 = bf16[128,512]{1,0:T(8,128)(2,1)S(1)} collective-permute-done((bf16[128,512]{1,0:T(8,128)(2,1)S(1)}, bf16[128,512]{1,0:T(8,128)(2,1)S(1)}, u32[]{:S(2)}, u32[]{:S(2)}) %collective-permute-start.33) | collective-permute-done | bytes 131104 | tf_op jit(solution)/shard_map/ppermute | solution.py:20
  123.9 2.8 collective-permute-start.39
  126.7 3.1 %pull.3.refs_2_ = f32[2,256,256]{2,1,0:T(8,128)} custom-call(bf16[128,2048]{1,0:T(8,128)(2,1)} %copy-done.9, bf16[128,2048]{1,0:T(8,128)(2,1)} %collective-permute-done.28.refs_1_.refs_7_, bf16[3,224,2048]{2,1,0:T(8,128)(2,1)} %get-tuple-element.114.refs_6_.refs_2_.refs_5_, bf16[3,224,2048]{2,1,0:T(8,128)(2,1)} %copy-done.2), custom_call_target="tpu_custom_call" | custom-call | flops 1 | bytes 1 | tf_op jit(solution)/shard_map/pull/pallas_call | solution.py:77
  129.9 2.1 collective-permute-done.35.refs_3_
  132.8 11.5 %slots.1 = (bf16[128,2048]{1,0:T(8,128)(2,1)}, bf16[128,2048]{1,0:T(8,128)(2,1)}, bf16[128,2048]{1,0:T(8,128)(2,1)}, bf16[128,2048]{1,0:T(8,128)(2,1)}, bf16[128...) custom-call(f32[2,768,256]{2,1,0:T(8,128)} %pull.2.refs_0_, ...), custom_call_target="tpu_custom_call" | custom-call | flops 1 | bytes 1 | tf_op jit(solution)/shard_map/slots/pallas_call | solution.py:167
  144.4 3.2 %collective-permute-start.37 = (bf16[128,2048]{1,0:T(8,128)(2,1)}, bf16[128,2048]{1,0:T(8,128)(2,1)S(1)}, u32[]{:S(2)}, u32[]{:S(2)}) collective-permute-start(bf16[128,2048]{1,0:T(8,128)(2,1)} %get-tuple-element.123), channel_id=1, source_target_pairs={{0,3},{1,0},{2,1},{3,2},{4,7},{5,4},{6,5},{7,6},{8,11},{9,8},{10,9... | collective-permute-start | bytes 1572872 | tf_op jit(solution)/shard_map/ppermute | solution.py:20
  148.9 3.2 %collective-permute-done.38.refs_2_.refs_10_ = bf16[256,2176]{1,0:T(8,128)(2,1)S(1)} collective-permute-done((bf16[256,2176]{1,0:T(8,128)(2,1)S(1)}, bf16[256,2176]{1,0:T(8,128)(2,1)S(1)}, u32[]{:S(2)}, u32[]{:S(2)}) %collective-permute-start.38) | collective-permute-done | bytes 1114144 | tf_op jit(solution)/shard_map/ppermute | solution.py:20
  152.1 3.2 %collective-permute-start.45 = (f32[256]{0:T(256)S(1)}, f32[256]{0:T(256)S(1)}, u32[]{:S(2)}, u32[]{:S(2)}) collective-permute-start(f32[256]{0:T(256)S(1)} %get-tuple-element.179), channel_id=1, source_target_pairs={{0,3},{1,0},{2,1},{3,2},{4,7},{5,4},{6,5},{7,6},{8,11},{9,8},{10,9... | collective-permute-start | bytes 3080 | tf_op jit(solution)/shard_map/ppermute | solution.py:20
  155.3 8.0 %collective-permute-done.36 = bf16[128,2048]{1,0:T(8,128)(2,1)S(1)} collective-permute-done((bf16[128,2048]{1,0:T(8,128)(2,1)}, bf16[128,2048]{1,0:T(8,128)(2,1)S(1)}, u32[]{:S(2)}, u32[]{:S(2)}) %collective-permute-start.36) | collective-permute-done | bytes 524320 | tf_op jit(solution)/shard_map/ppermute | solution.py:20
  165.6 1.4 collective-permute-start.43
  167.9 5.0 %collective-permute-done.44 = f32[256]{0:T(256)S(1)} collective-permute-done((f32[256]{0:T(256)S(1)}, f32[256]{0:T(256)S(1)}, u32[]{:S(2)}, u32[]{:S(2)}) %collective-permute-start.44) | collective-permute-done | bytes 1056 | tf_op jit(solution)/shard_map/ppermute | solution.py:20
  174.5 2.8 collective-permute-done.47
  180.1 1.6 collective-permute-done.48
  181.8 2.9 collective-permute-start.54
  184.7 1.6 add_convert_fusion
  189.6 3.2 %collective-permute-start.57 = (f32[2,32]{1,0:T(2,128)S(1)}, f32[2,32]{1,0:T(2,128)S(1)}, u32[]{:S(2)}, u32[]{:S(2)}) collective-permute-start(f32[2,32]{1,0:T(2,128)S(1)} %bitcast.117), channel_id=1, source_target_pairs={{0,8},{8,16},{16,24},{24,0},{1,9},{9,17},{17,25},{25,1},{2,10},{10... | collective-permute-start | bytes 776 | tf_op jit(solution)/shard_map/ppermute | solution.py:20
  195.1 2.7 collective-permute-done.56
  197.8 3.2 %collective-permute-start.53 = (bf16[128,2176]{1,0:T(8,128)(2,1)S(1)}, bf16[128,2176]{1,0:T(8,128)(2,1)S(1)}, u32[]{:S(2)}, u32[]{:S(2)}) collective-permute-start(bf16[128,2176]{1,0:T(8,128)(2,1)S(1)} %slice.249), channel_id=1, source_target_pairs={{0,3},{1,0},{2,1},{3,2},{4,7},{5,4},{6,5},{7,6},{8,11},{9,8},{10,9... | collective-permute-start | bytes 1671176 | tf_op jit(solution)/shard_map/ppermute | solution.py:20
  202.5 6.3 %collective-permute-done.52.refs_3_.refs_11_ = bf16[128,2176]{1,0:T(8,128)(2,1)S(1)} collective-permute-done((bf16[128,2176]{1,0:T(8,128)(2,1)}, bf16[128,2176]{1,0:T(8,128)(2,1)S(1)}, u32[]{:S(2)}, u32[]{:S(2)}) %collective-permute-start.52) | collective-permute-done | bytes 557088 | tf_op jit(solution)/shard_map/ppermute | solution.py:20
  210.2 3.0 %collective-permute-start.61 = (bf16[128,512]{1,0:T(8,128)(2,1)S(1)}, bf16[128,512]{1,0:T(8,128)(2,1)S(1)}, u32[]{:S(2)}, u32[]{:S(2)}) collective-permute-start(bf16[128,512]{1,0:T(8,128)(2,1)S(1)} %add_convert_fusion.4), channel_id=1, source_target_pairs={{0,4},{4,0},{1,5},{5,1},{2,6},{6,2},{3,7},{7,3},{8,12},{12,8},{9,1... | collective-permute-start | bytes 393224 | tf_op jit(solution)/shard_map/ppermute | solution.py:24
  213.2 8.0 %grads.2 = (bf16[224,2048]{1,0:T(8,128)(2,1)}, bf16[224,2048]{1,0:T(8,128)(2,1)}, bf16[224,2048]{1,0:T(8,128)(2,1)}, bf16[224,2048]{1,0:T(8,128)(2,1)}, f32[8,512]{1,0:T(8,128)}) custom-call(bf16[256,2176]{1,0:T(8,128)(2,1)} %copy-done.3, bf16[256,2176]{1,0:T(8,128)(2,1)} %copy-done.5, bf16[256,2176]{1,0:T(8,128)(2,1)} %copy-done.4, ...), custom_call_target="tpu_custom_call" | custom-call | flops 1 | bytes 1 | tf_op jit(solution)/shard_map/grads/pallas_call | solution.py:282
  221.2 2.9 collective-permute-start.58
  224.1 1.7 collective-permute-start.60
  225.8 6.6 %grads.3 = (bf16[224,2048]{1,0:T(8,128)(2,1)}, bf16[224,2048]{1,0:T(8,128)(2,1)}, f32[8,512]{1,0:T(8,128)}) custom-call(bf16[128,2048]{1,0:T(8,128)(2,1)} %copy-done.6, bf16[128,2048]{1,0:T(8,128)(2,1)} %pad_maximum_fusion.3.refs_1_, bf16[128,2048]{1,0:T(8,128)(2,1)} %collective-permute-done.22.refs_2_, bf16[128,2048]{1,0:T(8,128)(2,1)} %collective-permute-done.25.refs_3_, ...), custom_call_target="tpu_custom_call" | custom-call | flops 1 | bytes 1 | tf_op jit(solution)/shard_map/grads/pallas_call | solution.py:282
  233.4 3.2 %collective-permute-start.64 = (f32[16,512]{1,0:T(8,128)S(1)}, f32[16,512]{1,0:T(8,128)S(1)}, u32[]{:S(2)}, u32[]{:S(2)}) collective-permute-start(f32[16,512]{1,0:T(8,128)S(1)} %pad_maximum_fusion.13), channel_id=1, source_target_pairs={{0,3},{1,0},{2,1},{3,2},{4,7},{5,4},{6,5},{7,6},{8,11},{9,8},{10,9... | collective-permute-start | bytes 98312 | tf_op jit(solution)/shard_map/ppermute | solution.py:20
  238.5 3.5 %collective-permute-done.62 = f32[16,512]{1,0:T(8,128)S(1)} collective-permute-done((f32[16,512]{1,0:T(8,128)S(1)}, f32[16,512]{1,0:T(8,128)S(1)}, u32[]{:S(2)}, u32[]{:S(2)}) %collective-permute-start.62) | collective-permute-done | bytes 32800 | tf_op jit(solution)/shard_map/ppermute | solution.py:20
  244.6 2.3 collective-permute-start.67
  247.0 2.1 collective-permute-start.66
  249.6 3.1 %collective-permute-done.66 = bf16[2,32,512]{2,1,0:T(8,128)(2,1)S(1)} collective-permute-done((bf16[2,32,512]{2,1,0:T(8,128)(2,1)S(1)}, bf16[2,32,512]{2,1,0:T(8,128)(2,1)S(1)}, u32[]{:S(2)}, u32[]{:S(2)}) %collective-permute-start.66) | collective-permute-done | bytes 65568 | tf_op jit(solution)/shard_map/ppermute | solution.py:20
  252.8 1.8 collective-permute-done.65
  254.6 3.4 %collective-permute-start.71 = (f32[16,512]{1,0:T(8,128)S(1)}, f32[16,512]{1,0:T(8,128)S(1)}, u32[]{:S(2)}, u32[]{:S(2)}) collective-permute-start(f32[16,512]{1,0:T(8,128)S(1)} %add_add_fusion), channel_id=1, source_target_pairs={{0,4},{4,0},{1,5},{5,1},{2,6},{6,2},{3,7},{7,3},{8,12},{12,8},{9,1... | collective-permute-start | bytes 98312 | tf_op jit(solution)/shard_map/ppermute | solution.py:24
  258.0 4.5 %collective-permute-done.71 = f32[16,512]{1,0:T(8,128)S(1)} collective-permute-done((f32[16,512]{1,0:T(8,128)S(1)}, f32[16,512]{1,0:T(8,128)S(1)}, u32[]{:S(2)}, u32[]{:S(2)}) %collective-permute-start.71) | collective-permute-done | bytes 32800 | tf_op jit(solution)/shard_map/ppermute | solution.py:24
  265.7 2.4 collective-permute-start.74
  269.1 1.8 collective-permute-start.75
  272.8 3.1 %collective-permute-done.73 = f32[8,128]{1,0:T(8,128)S(1)} collective-permute-done((f32[8,128]{1,0:T(8,128)S(1)}, f32[8,128]{1,0:T(8,128)S(1)}, u32[]{:S(2)}, u32[]{:S(2)}) %collective-permute-start.73) | collective-permute-done | bytes 4128 | tf_op jit(solution)/shard_map/ppermute | solution.py:20
  280.0 6.5 %finish.1 = (bf16[1,224,4096]{2,1,0:T(8,128)(2,1)}, bf16[1,224,4096]{2,1,0:T(8,128)(2,1)}, bf16[1,224,4096]{2,1,0:T(8,128)(2,1)}) custom-call(s32[5]{0:T(128)} %stack.41.place, f32[1]{0:T(128)} %bitcast.53.factor, bf16[224,2048]{1,0:T(8,128)(2,1)} %get-tuple-element.168.refs_0_, bf16[224,2048]{1,0:T(8,128)(2,1)} %copy-done.10, ...), custom_call_target="tpu_custom_call" | custom-call | flops 1 | bytes 1 | tf_op jit(solution)/shard_map/finish/pallas_call | solution.py:234
  (250 shorter events, 55.6 us)
Async XLA Ops:
  2.5 19.4 %collective-permute-start.2 = (bf16[32,512]{1,0:T(8,128)(2,1)S(1)}, bf16[32,512]{1,0:T(8,128)(2,1)S(1)}, u32[]{:S(2)}, u32[]{:S(2)}) collective-permute-start(bf16[32,512]{1,0:T(8,128)(2,1)S(1)} %get-tuple-element.204), channel_id=1, source_target_pairs={{0,24},{8,0},{16,8},{24,16},{1,25},{9,1},{17,9},{25,17},{2,26},{10... | collective-permute-start | bytes 98312 | tf_op jit(solution)/shard_map/ppermute | solution.py:20
  3.4 18.5 %collective-permute-start.1 = (bf16[32,512]{1,0:T(8,128)(2,1)S(1)}, bf16[32,512]{1,0:T(8,128)(2,1)S(1)}, u32[]{:S(2)}, u32[]{:S(2)}) collective-permute-start(bf16[32,512]{1,0:T(8,128)(2,1)S(1)} %get-tuple-element.205), channel_id=1, source_target_pairs={{0,16},{8,24},{16,0},{24,8},{1,17},{9,25},{17,1},{25,9},{2,18},{10... | collective-permute-start | bytes 98312 | tf_op jit(solution)/shard_map/ppermute | solution.py:20
  6.3 15.7 %collective-permute-start = (bf16[32,512]{1,0:T(8,128)(2,1)S(1)}, bf16[32,512]{1,0:T(8,128)(2,1)S(1)}, u32[]{:S(2)}, u32[]{:S(2)}) collective-permute-start(bf16[32,512]{1,0:T(8,128)(2,1)S(1)} %get-tuple-element.206), channel_id=1, source_target_pairs={{0,8},{8,16},{16,24},{24,0},{1,9},{9,17},{17,25},{25,1},{2,10},{10... | collective-permute-start | bytes 98312 | tf_op jit(solution)/shard_map/ppermute | solution.py:20
  6.7 15.4 %collective-permute-start.3 = (bf16[128,512]{1,0:T(8,128)(2,1)S(1)}, bf16[128,512]{1,0:T(8,128)(2,1)S(1)}, u32[]{:S(2)}, u32[]{:S(2)}) collective-permute-start(bf16[128,512]{1,0:T(8,128)(2,1)S(1)} %slice.279), channel_id=1, source_target_pairs={{0,4},{4,0},{1,5},{5,1},{2,6},{6,2},{3,7},{7,3},{8,12},{12,8},{9,1... | collective-permute-start | bytes 393224 | tf_op jit(solution)/shard_map/ppermute | solution.py:24
  15.0 7.0 %collective-permute-start.4 = (f32[128,8]{0,1:T(8,128)S(1)}, f32[128,8]{0,1:T(8,128)S(1)}, u32[]{:S(2)}, u32[]{:S(2)}) collective-permute-start(f32[128,8]{0,1:T(8,128)S(1)} %convolution_bitcast_fusion), channel_id=1, source_target_pairs={{0,32},{32,0},{1,33},{33,1},{2,34},{34,2},{3,35},{35,3},{4,36},{36... | collective-permute-start | bytes 12296 | tf_op jit(solution)/shard_map/ppermute | solution.py:24
  23.2 20.8 %collective-permute-start.9 = (bf16[128,512]{1,0:T(8,128)(2,1)S(1)}, bf16[128,512]{1,0:T(8,128)(2,1)S(1)}, u32[]{:S(2)}, u32[]{:S(2)}) collective-permute-start(bf16[128,512]{1,0:T(8,128)(2,1)S(1)} %pad_maximum_fusion.9), channel_id=1, source_target_pairs={{0,192},{64,0},{128,64},{192,128},{1,193},{65,1},{129,65},{193,129... | collective-permute-start | bytes 393224 | tf_op jit(solution)/shard_map/ppermute | solution.py:20
  25.1 18.9 %collective-permute-start.8 = (bf16[128,512]{1,0:T(8,128)(2,1)S(1)}, bf16[128,512]{1,0:T(8,128)(2,1)S(1)}, u32[]{:S(2)}, u32[]{:S(2)}) collective-permute-start(bf16[128,512]{1,0:T(8,128)(2,1)S(1)} %pad_maximum_fusion.9), channel_id=1, source_target_pairs={{0,128},{64,192},{128,0},{192,64},{1,129},{65,193},{129,1},{193,65... | collective-permute-start | bytes 393224 | tf_op jit(solution)/shard_map/ppermute | solution.py:20
  25.6 18.4 %collective-permute-start.7 = (bf16[128,512]{1,0:T(8,128)(2,1)S(1)}, bf16[128,512]{1,0:T(8,128)(2,1)S(1)}, u32[]{:S(2)}, u32[]{:S(2)}) collective-permute-start(bf16[128,512]{1,0:T(8,128)(2,1)S(1)} %pad_maximum_fusion.9), channel_id=1, source_target_pairs={{0,64},{64,128},{128,192},{192,0},{1,65},{65,129},{129,193},{193,1... | collective-permute-start | bytes 393224 | tf_op jit(solution)/shard_map/ppermute | solution.py:20
  26.7 11.1 %collective-permute-start.6 = (f32[128,8]{0,1:T(8,128)S(1)}, f32[128,8]{0,1:T(8,128)S(1)}, u32[]{:S(2)}, u32[]{:S(2)}) collective-permute-start(f32[128,8]{0,1:T(8,128)S(1)} %add.340), channel_id=1, source_target_pairs={{0,128},{64,192},{128,0},{192,64},{1,129},{65,193},{129,1},{193,65... | collective-permute-start | bytes 12296 | tf_op jit(solution)/shard_map/ppermute | solution.py:29
  28.1 11.8 %collective-permute-start.12 = (bf16[32,512]{1,0:T(8,128)(2,1)S(1)}, bf16[32,512]{1,0:T(8,128)(2,1)S(1)}, u32[]{:S(2)}, u32[]{:S(2)}) collective-permute-start(bf16[32,512]{1,0:T(8,128)(2,1)S(1)} %get-tuple-element.208), channel_id=1, source_target_pairs={{0,24},{8,0},{16,8},{24,16},{1,25},{9,1},{17,9},{25,17},{2,26},{10... | collective-permute-start | bytes 98312 | tf_op jit(solution)/shard_map/ppermute | solution.py:20
  37.8 5.4 %collective-permute-start.11 = (bf16[32,512]{1,0:T(8,128)(2,1)S(1)}, bf16[32,512]{1,0:T(8,128)(2,1)S(1)}, u32[]{:S(2)}, u32[]{:S(2)}) collective-permute-start(bf16[32,512]{1,0:T(8,128)(2,1)S(1)} %get-tuple-element.209), channel_id=1, source_target_pairs={{0,16},{8,24},{16,0},{24,8},{1,17},{9,25},{17,1},{25,9},{2,18},{10... | collective-permute-start | bytes 98312 | tf_op jit(solution)/shard_map/ppermute | solution.py:20
  44.1 24.8 %collective-permute-start.20 = (bf16[3,224,2048]{2,1,0:T(8,128)(2,1)}, bf16[3,224,2048]{2,1,0:T(8,128)(2,1)S(1)}, u32[]{:S(2)}, u32[]{:S(2)}) collective-permute-start(bf16[3,224,2048]{2,1,0:T(8,128)(2,1)} %get-tuple-element.105), channel_id=1, source_target_pairs={{0,32},{32,0},{1,33},{33,1},{2,34},{34,2},{3,35},{35,3},{4,36},{36... | collective-permute-start | bytes 8257544 | tf_op jit(solution)/shard_map/ppermute | solution.py:24
  44.3 17.0 %collective-permute-start.15 = (bf16[128,512]{1,0:T(8,128)(2,1)S(1)}, bf16[128,512]{1,0:T(8,128)(2,1)S(1)}, u32[]{:S(2)}, u32[]{:S(2)}) collective-permute-start(bf16[128,512]{1,0:T(8,128)(2,1)S(1)} %pad_maximum_fusion.10), channel_id=1, source_target_pairs={{0,192},{64,0},{128,64},{192,128},{1,193},{65,1},{129,65},{193,129... | collective-permute-start | bytes 393224 | tf_op jit(solution)/shard_map/ppermute | solution.py:20
  47.6 15.4 %collective-permute-start.14 = (bf16[128,512]{1,0:T(8,128)(2,1)S(1)}, bf16[128,512]{1,0:T(8,128)(2,1)S(1)}, u32[]{:S(2)}, u32[]{:S(2)}) collective-permute-start(bf16[128,512]{1,0:T(8,128)(2,1)S(1)} %pad_maximum_fusion.10), channel_id=1, source_target_pairs={{0,128},{64,192},{128,0},{192,64},{1,129},{65,193},{129,1},{193,65... | collective-permute-start | bytes 393224 | tf_op jit(solution)/shard_map/ppermute | solution.py:20
  47.6 6.8 %collective-permute-start.18 = (bf16[2,32,640]{2,1,0:T(8,128)(2,1)S(1)}, bf16[2,32,640]{2,1,0:T(8,128)(2,1)S(1)}, u32[]{:S(2)}, u32[]{:S(2)}) collective-permute-start(bf16[2,32,640]{2,1,0:T(8,128)(2,1)S(1)} %get-tuple-element.197), channel_id=1, source_target_pairs={{0,24},{8,0},{16,8},{24,16},{1,25},{9,1},{17,9},{25,17},{2,26},{10... | collective-permute-start | bytes 245768 | tf_op jit(solution)/shard_map/ppermute | solution.py:20
  48.0 7.5 %collective-permute-start.17 = (bf16[2,32,640]{2,1,0:T(8,128)(2,1)S(1)}, bf16[2,32,640]{2,1,0:T(8,128)(2,1)S(1)}, u32[]{:S(2)}, u32[]{:S(2)}) collective-permute-start(bf16[2,32,640]{2,1,0:T(8,128)(2,1)S(1)} %get-tuple-element.196), channel_id=1, source_target_pairs={{0,16},{8,24},{16,0},{24,8},{1,17},{9,25},{17,1},{25,9},{2,18},{10... | collective-permute-start | bytes 245768 | tf_op jit(solution)/shard_map/ppermute | solution.py:20
  54.4 13.2 %collective-permute-start.19 = (bf16[2,224,1024]{2,1,0:T(8,128)(2,1)S(1)}, bf16[2,224,1024]{2,1,0:T(8,128)(2,1)S(1)}, u32[]{:S(2)}, u32[]{:S(2)}) collective-permute-start(bf16[2,224,1024]{2,1,0:T(8,128)(2,1)S(1)} %pad_maximum_fusion.1), channel_id=1, source_target_pairs={{0,32},{32,0},{1,33},{33,1},{2,34},{34,2},{3,35},{35,3},{4,36},{36... | collective-permute-start | bytes 2752520 | tf_op jit(solution)/shard_map/ppermute | solution.py:24
  59.9 6.8 %collective-permute-start.13 = (bf16[128,512]{1,0:T(8,128)(2,1)S(1)}, bf16[128,512]{1,0:T(8,128)(2,1)S(1)}, u32[]{:S(2)}, u32[]{:S(2)}) collective-permute-start(bf16[128,512]{1,0:T(8,128)(2,1)S(1)} %pad_maximum_fusion.10), channel_id=1, source_target_pairs={{0,64},{64,128},{128,192},{192,0},{1,65},{65,129},{129,193},{193,1... | collective-permute-start | bytes 393224 | tf_op jit(solution)/shard_map/ppermute | solution.py:20
  61.4 16.2 %collective-permute-start.21 = (bf16[128,2048]{1,0:T(8,128)(2,1)S(1)}, bf16[128,2048]{1,0:T(8,128)(2,1)}, u32[]{:S(2)}, u32[]{:S(2)}) collective-permute-start(bf16[128,2048]{1,0:T(8,128)(2,1)S(1)} %pad_maximum_fusion.2.refs_0_), channel_id=1, source_target_pairs={{0,1},{1,2},{2,3},{3,0},{4,5},{5,6},{6,7},{7,4},{8,9},{9,10},{10,1... | collective-permute-start | bytes 1572872 | tf_op jit(solution)/shard_map/ppermute | solution.py:20
  62.9 16.6 %collective-permute-start.22 = (bf16[128,2048]{1,0:T(8,128)(2,1)S(1)}, bf16[128,2048]{1,0:T(8,128)(2,1)}, u32[]{:S(2)}, u32[]{:S(2)}) collective-permute-start(bf16[128,2048]{1,0:T(8,128)(2,1)S(1)} %pad_maximum_fusion.2.refs_0_), channel_id=1, source_target_pairs={{0,3},{1,0},{2,1},{3,2},{4,7},{5,4},{6,5},{7,6},{8,11},{9,8},{10,9... | collective-permute-start | bytes 1572872 | tf_op jit(solution)/shard_map/ppermute | solution.py:20
  69.0 21.4 %collective-permute-start.24 = (bf16[128,2048]{1,0:T(8,128)(2,1)}, bf16[128,2048]{1,0:T(8,128)(2,1)}, u32[]{:S(2)}, u32[]{:S(2)}) collective-permute-start(bf16[128,2048]{1,0:T(8,128)(2,1)} %pad_maximum_fusion.3.refs_1_), channel_id=1, source_target_pairs={{0,1},{1,2},{2,3},{3,0},{4,5},{5,6},{6,7},{7,4},{8,9},{9,10},{10,1... | collective-permute-start | bytes 1572872 | tf_op jit(solution)/shard_map/ppermute | solution.py:20
  70.5 19.8 %collective-permute-start.25 = (bf16[128,2048]{1,0:T(8,128)(2,1)}, bf16[128,2048]{1,0:T(8,128)(2,1)}, u32[]{:S(2)}, u32[]{:S(2)}) collective-permute-start(bf16[128,2048]{1,0:T(8,128)(2,1)} %pad_maximum_fusion.3.refs_1_), channel_id=1, source_target_pairs={{0,3},{1,0},{2,1},{3,2},{4,7},{5,4},{6,5},{7,6},{8,11},{9,8},{10,9... | collective-permute-start | bytes 1572872 | tf_op jit(solution)/shard_map/ppermute | solution.py:20
  73.1 35.1 %collective-permute-start.31 = (bf16[128,512]{1,0:T(8,128)(2,1)S(1)}, bf16[128,512]{1,0:T(8,128)(2,1)}, u32[]{:S(2)}, u32[]{:S(2)}) collective-permute-start(bf16[128,512]{1,0:T(8,128)(2,1)S(1)} %slice.237), channel_id=1, source_target_pairs={{0,192},{64,0},{128,64},{192,128},{1,193},{65,1},{129,65},{193,129... | collective-permute-start | bytes 393224 | tf_op jit(solution)/shard_map/ppermute | solution.py:20
  77.5 31.0 %collective-permute-start.30 = (bf16[128,512]{1,0:T(8,128)(2,1)S(1)}, bf16[128,512]{1,0:T(8,128)(2,1)}, u32[]{:S(2)}, u32[]{:S(2)}) collective-permute-start(bf16[128,512]{1,0:T(8,128)(2,1)S(1)} %slice.237), channel_id=1, source_target_pairs={{0,128},{64,192},{128,0},{192,64},{1,129},{65,193},{129,1},{193,65... | collective-permute-start | bytes 393224 | tf_op jit(solution)/shard_map/ppermute | solution.py:20
  79.5 10.8 %collective-permute-start.23 = (bf16[128,640]{1,0:T(8,128)(2,1)}, bf16[128,640]{1,0:T(8,128)(2,1)S(1)}, u32[]{:S(2)}, u32[]{:S(2)}) collective-permute-start(bf16[128,640]{1,0:T(8,128)(2,1)} %get-tuple-element.107), channel_id=1, source_target_pairs={{0,4},{4,0},{1,5},{5,1},{2,6},{6,2},{3,7},{7,3},{8,12},{12,8},{9,1... | collective-permute-start | bytes 491528 | tf_op jit(solution)/shard_map/ppermute | solution.py:24
  95.3 36.7 %collective-permute-start.26 = (f32[2,768,256]{2,1,0:T(8,128)}, f32[2,768,256]{2,1,0:T(8,128)}, u32[]{:S(2)}, u32[]{:S(2)}) collective-permute-start(f32[2,768,256]{2,1,0:T(8,128)} %pull.2.refs_0_), channel_id=1, source_target_pairs={{0,32},{32,0},{1,33},{33,1},{2,34},{34,2},{3,35},{35,3},{4,36},{36... | collective-permute-start | bytes 4718600 | tf_op jit(solution)/shard_map/ppermute | solution.py:24
  95.3 16.2 %collective-permute-start.29 = (bf16[128,512]{1,0:T(8,128)(2,1)S(1)}, bf16[128,512]{1,0:T(8,128)(2,1)S(1)}, u32[]{:S(2)}, u32[]{:S(2)}) collective-permute-start(bf16[128,512]{1,0:T(8,128)(2,1)S(1)} %slice.237), channel_id=1, source_target_pairs={{0,64},{64,128},{128,192},{192,0},{1,65},{65,129},{129,193},{193,1... | collective-permute-start | bytes 393224 | tf_op jit(solution)/shard_map/ppermute | solution.py:20
  98.0 14.6 %collective-permute-start.34 = (bf16[128,512]{1,0:T(8,128)(2,1)S(1)}, bf16[128,512]{1,0:T(8,128)(2,1)S(1)}, u32[]{:S(2)}, u32[]{:S(2)}) collective-permute-start(bf16[128,512]{1,0:T(8,128)(2,1)S(1)} %slice.238), channel_id=1, source_target_pairs={{0,192},{64,0},{128,64},{192,128},{1,193},{65,1},{129,65},{193,129... | collective-permute-start | bytes 393224 | tf_op jit(solution)/shard_map/ppermute | solution.py:20
  108.2 15.1 %collective-permute-start.27 = (bf16[128,2048]{1,0:T(8,128)(2,1)}, bf16[128,2048]{1,0:T(8,128)(2,1)S(1)}, u32[]{:S(2)}, u32[]{:S(2)}) collective-permute-start(bf16[128,2048]{1,0:T(8,128)(2,1)} %collective-permute-done.21.refs_4_), channel_id=1, source_target_pairs={{0,1},{1,2},{2,3},{3,0},{4,5},{5,6},{6,7},{7,4},{8,9},{9,10},{10,1... | collective-permute-start | bytes 1572872 | tf_op jit(solution)/shard_map/ppermute | solution.py:20
  108.5 14.8 %collective-permute-start.28 = (bf16[128,2048]{1,0:T(8,128)(2,1)}, bf16[128,2048]{1,0:T(8,128)(2,1)}, u32[]{:S(2)}, u32[]{:S(2)}) collective-permute-start(bf16[128,2048]{1,0:T(8,128)(2,1)} %collective-permute-done.25.refs_3_), channel_id=1, source_target_pairs={{0,3},{1,0},{2,1},{3,2},{4,7},{5,4},{6,5},{7,6},{8,11},{9,8},{10,9... | collective-permute-start | bytes 1572872 | tf_op jit(solution)/shard_map/ppermute | solution.py:20
  111.4 11.2 %collective-permute-start.33 = (bf16[128,512]{1,0:T(8,128)(2,1)S(1)}, bf16[128,512]{1,0:T(8,128)(2,1)S(1)}, u32[]{:S(2)}, u32[]{:S(2)}) collective-permute-start(bf16[128,512]{1,0:T(8,128)(2,1)S(1)} %slice.238), channel_id=1, source_target_pairs={{0,128},{64,192},{128,0},{192,64},{1,129},{65,193},{129,1},{193,65... | collective-permute-start | bytes 393224 | tf_op jit(solution)/shard_map/ppermute | solution.py:20
  112.5 10.1 %collective-permute-start.32 = (bf16[128,512]{1,0:T(8,128)(2,1)S(1)}, bf16[128,512]{1,0:T(8,128)(2,1)S(1)}, u32[]{:S(2)}, u32[]{:S(2)}) collective-permute-start(bf16[128,512]{1,0:T(8,128)(2,1)S(1)} %slice.238), channel_id=1, source_target_pairs={{0,64},{64,128},{128,192},{192,0},{1,65},{65,129},{129,193},{193,1... | collective-permute-start | bytes 393224 | tf_op jit(solution)/shard_map/ppermute | solution.py:20
  123.4 28.6 %collective-permute-start.38 = (bf16[256,2176]{1,0:T(8,128)(2,1)S(1)}, bf16[256,2176]{1,0:T(8,128)(2,1)S(1)}, u32[]{:S(2)}, u32[]{:S(2)}) collective-permute-start(bf16[256,2176]{1,0:T(8,128)(2,1)S(1)} %maximum_maximum_fusion.refs_0_.refs_8_), channel_id=1, source_target_pairs={{0,1},{1,2},{2,3},{3,0},{4,5},{5,6},{6,7},{7,4},{8,9},{9,10},{10,1... | collective-permute-start | bytes 3342344 | tf_op jit(solution)/shard_map/ppermute | solution.py:20
  123.9 28.2 %collective-permute-start.39 = (bf16[256,2176]{1,0:T(8,128)(2,1)S(1)}, bf16[256,2176]{1,0:T(8,128)(2,1)S(1)}, u32[]{:S(2)}, u32[]{:S(2)}) collective-permute-start(bf16[256,2176]{1,0:T(8,128)(2,1)S(1)} %maximum_maximum_fusion.refs_0_.refs_8_), channel_id=1, source_target_pairs={{0,3},{1,0},{2,1},{3,2},{4,7},{5,4},{6,5},{7,6},{8,11},{9,8},{10,9... | collective-permute-start | bytes 3342344 | tf_op jit(solution)/shard_map/ppermute | solution.py:20
  144.3 19.0 %collective-permute-start.36 = (bf16[128,2048]{1,0:T(8,128)(2,1)}, bf16[128,2048]{1,0:T(8,128)(2,1)S(1)}, u32[]{:S(2)}, u32[]{:S(2)}) collective-permute-start(bf16[128,2048]{1,0:T(8,128)(2,1)} %get-tuple-element.122), channel_id=1, source_target_pairs={{0,1},{1,2},{2,3},{3,0},{4,5},{5,6},{6,7},{7,4},{8,9},{9,10},{10,1... | collective-permute-start | bytes 1572872 | tf_op jit(solution)/shard_map/ppermute | solution.py:20
  144.4 20.0 %collective-permute-start.37 = (bf16[128,2048]{1,0:T(8,128)(2,1)}, bf16[128,2048]{1,0:T(8,128)(2,1)S(1)}, u32[]{:S(2)}, u32[]{:S(2)}) collective-permute-start(bf16[128,2048]{1,0:T(8,128)(2,1)} %get-tuple-element.123), channel_id=1, source_target_pairs={{0,3},{1,0},{2,1},{3,2},{4,7},{5,4},{6,5},{7,6},{8,11},{9,8},{10,9... | collective-permute-start | bytes 1572872 | tf_op jit(solution)/shard_map/ppermute | solution.py:20
  147.6 34.2 %collective-permute-start.42 = (bf16[128,2048]{1,0:T(8,128)(2,1)}, bf16[128,2048]{1,0:T(8,128)(2,1)}, u32[]{:S(2)}, u32[]{:S(2)}) collective-permute-start(bf16[128,2048]{1,0:T(8,128)(2,1)} %get-tuple-element.130), channel_id=1, source_target_pairs={{0,1},{1,2},{2,3},{3,0},{4,5},{5,6},{6,7},{7,4},{8,9},{9,10},{10,1... | collective-permute-start | bytes 1572872 | tf_op jit(solution)/shard_map/ppermute | solution.py:20
  152.1 20.9 %collective-permute-start.44 = (f32[256]{0:T(256)S(1)}, f32[256]{0:T(256)S(1)}, u32[]{:S(2)}, u32[]{:S(2)}) collective-permute-start(f32[256]{0:T(256)S(1)} %get-tuple-element.180), channel_id=1, source_target_pairs={{0,1},{1,2},{2,3},{3,0},{4,5},{5,6},{6,7},{7,4},{8,9},{9,10},{10,1... | collective-permute-start | bytes 3080 | tf_op jit(solution)/shard_map/ppermute | solution.py:20
  152.1 20.8 %collective-permute-start.45 = (f32[256]{0:T(256)S(1)}, f32[256]{0:T(256)S(1)}, u32[]{:S(2)}, u32[]{:S(2)}) collective-permute-start(f32[256]{0:T(256)S(1)} %get-tuple-element.179), channel_id=1, source_target_pairs={{0,3},{1,0},{2,1},{3,2},{4,7},{5,4},{6,5},{7,6},{8,11},{9,8},{10,9... | collective-permute-start | bytes 3080 | tf_op jit(solution)/shard_map/ppermute | solution.py:20
  163.3 10.4 %collective-permute-start.46 = (f32[256]{0:T(256)S(1)}, f32[256]{0:T(256)S(1)}, u32[]{:S(2)}, u32[]{:S(2)}) collective-permute-start(f32[256]{0:T(256)S(1)} %get-tuple-element.178), channel_id=1, source_target_pairs={{0,2},{1,3},{2,0},{3,1},{4,6},{5,7},{6,4},{7,5},{8,10},{9,11},{10,... | collective-permute-start | bytes 3080 | tf_op jit(solution)/shard_map/ppermute | solution.py:20
  165.6 16.3 %collective-permute-start.43 = (bf16[128,2048]{1,0:T(8,128)(2,1)S(1)}, bf16[128,2048]{1,0:T(8,128)(2,1)}, u32[]{:S(2)}, u32[]{:S(2)}) collective-permute-start(bf16[128,2048]{1,0:T(8,128)(2,1)S(1)} %add_convert_fusion.1), channel_id=1, source_target_pairs={{0,3},{1,0},{2,1},{3,2},{4,7},{5,4},{6,5},{7,6},{8,11},{9,8},{10,9... | collective-permute-start | bytes 1572872 | tf_op jit(solution)/shard_map/ppermute | solution.py:20
  178.1 14.7 %collective-permute-start.41 = (bf16[128,2048]{1,0:T(8,128)(2,1)}, bf16[128,2048]{1,0:T(8,128)(2,1)S(1)}, u32[]{:S(2)}, u32[]{:S(2)}) collective-permute-start(bf16[128,2048]{1,0:T(8,128)(2,1)} %get-tuple-element.128), channel_id=1, source_target_pairs={{0,3},{1,0},{2,1},{3,2},{4,7},{5,4},{6,5},{7,6},{8,11},{9,8},{10,9... | collective-permute-start | bytes 1572872 | tf_op jit(solution)/shard_map/ppermute | solution.py:20
  178.8 13.9 %collective-permute-start.40 = (bf16[128,2048]{1,0:T(8,128)(2,1)}, bf16[128,2048]{1,0:T(8,128)(2,1)}, u32[]{:S(2)}, u32[]{:S(2)}) collective-permute-start(bf16[128,2048]{1,0:T(8,128)(2,1)} %add_convert_fusion.3), channel_id=1, source_target_pairs={{0,1},{1,2},{2,3},{3,0},{4,5},{5,6},{6,7},{7,4},{8,9},{9,10},{10,1... | collective-permute-start | bytes 1572872 | tf_op jit(solution)/shard_map/ppermute | solution.py:20
  181.8 7.8 %collective-permute-start.54 = (f32[4,32]{1,0:T(4,128)S(1)}, f32[4,32]{1,0:T(4,128)S(1)}, u32[]{:S(2)}, u32[]{:S(2)}) collective-permute-start(f32[4,32]{1,0:T(4,128)S(1)} %get-tuple-element.230), channel_id=1, source_target_pairs={{0,4},{4,0},{1,5},{5,1},{2,6},{6,2},{3,7},{7,3},{8,12},{12,8},{9,1... | collective-permute-start | bytes 1544 | tf_op jit(solution)/shard_map/ppermute | solution.py:24
  187.0 15.4 %collective-permute-start.49 = (bf16[128,512]{1,0:T(8,128)(2,1)}, bf16[128,512]{1,0:T(8,128)(2,1)S(1)}, u32[]{:S(2)}, u32[]{:S(2)}) collective-permute-start(bf16[128,512]{1,0:T(8,128)(2,1)} %get-tuple-element.192), channel_id=1, source_target_pairs={{0,192},{64,0},{128,64},{192,128},{1,193},{65,1},{129,65},{193,129... | collective-permute-start | bytes 393224 | tf_op jit(solution)/shard_map/ppermute | solution.py:20
  188.2 14.3 %collective-permute-start.50 = (bf16[128,512]{1,0:T(8,128)(2,1)}, bf16[128,512]{1,0:T(8,128)(2,1)}, u32[]{:S(2)}, u32[]{:S(2)}) collective-permute-start(bf16[128,512]{1,0:T(8,128)(2,1)} %get-tuple-element.191), channel_id=1, source_target_pairs={{0,128},{64,192},{128,0},{192,64},{1,129},{65,193},{129,1},{193,65... | collective-permute-start | bytes 393224 | tf_op jit(solution)/shard_map/ppermute | solution.py:20
  194.1 8.4 %collective-permute-start.51 = (bf16[128,512]{1,0:T(8,128)(2,1)}, bf16[128,512]{1,0:T(8,128)(2,1)}, u32[]{:S(2)}, u32[]{:S(2)}) collective-permute-start(bf16[128,512]{1,0:T(8,128)(2,1)} %get-tuple-element.190), channel_id=1, source_target_pairs={{0,64},{64,128},{128,192},{192,0},{1,65},{65,129},{129,193},{193,1... | collective-permute-start | bytes 393224 | tf_op jit(solution)/shard_map/ppermute | solution.py:20
  197.8 11.0 %collective-permute-start.52 = (bf16[128,2176]{1,0:T(8,128)(2,1)}, bf16[128,2176]{1,0:T(8,128)(2,1)S(1)}, u32[]{:S(2)}, u32[]{:S(2)}) collective-permute-start(bf16[128,2176]{1,0:T(8,128)(2,1)} %slice.248), channel_id=1, source_target_pairs={{0,1},{1,2},{2,3},{3,0},{4,5},{5,6},{6,7},{7,4},{8,9},{9,10},{10,1... | collective-permute-start | bytes 1671176 | tf_op jit(solution)/shard_map/ppermute | solution.py:20
  197.8 11.0 %collective-permute-start.53 = (bf16[128,2176]{1,0:T(8,128)(2,1)S(1)}, bf16[128,2176]{1,0:T(8,128)(2,1)S(1)}, u32[]{:S(2)}, u32[]{:S(2)}) collective-permute-start(bf16[128,2176]{1,0:T(8,128)(2,1)S(1)} %slice.249), channel_id=1, source_target_pairs={{0,3},{1,0},{2,1},{3,2},{4,7},{5,4},{6,5},{7,6},{8,11},{9,8},{10,9... | collective-permute-start | bytes 1671176 | tf_op jit(solution)/shard_map/ppermute | solution.py:20
  210.2 31.8 %collective-permute-start.61 = (bf16[128,512]{1,0:T(8,128)(2,1)S(1)}, bf16[128,512]{1,0:T(8,128)(2,1)S(1)}, u32[]{:S(2)}, u32[]{:S(2)}) collective-permute-start(bf16[128,512]{1,0:T(8,128)(2,1)S(1)} %add_convert_fusion.4), channel_id=1, source_target_pairs={{0,4},{4,0},{1,5},{5,1},{2,6},{6,2},{3,7},{7,3},{8,12},{12,8},{9,1... | collective-permute-start | bytes 393224 | tf_op jit(solution)/shard_map/ppermute | solution.py:24
  221.2 11.4 %collective-permute-start.58 = (bf16[128,512]{1,0:T(8,128)(2,1)S(1)}, bf16[128,512]{1,0:T(8,128)(2,1)S(1)}, u32[]{:S(2)}, u32[]{:S(2)}) collective-permute-start(bf16[128,512]{1,0:T(8,128)(2,1)S(1)} %get-tuple-element.189), channel_id=1, source_target_pairs={{0,192},{64,0},{128,64},{192,128},{1,193},{65,1},{129,65},{193,129... | collective-permute-start | bytes 393224 | tf_op jit(solution)/shard_map/ppermute | solution.py:20
  224.1 8.5 %collective-permute-start.59 = (bf16[128,512]{1,0:T(8,128)(2,1)S(1)}, bf16[128,512]{1,0:T(8,128)(2,1)S(1)}, u32[]{:S(2)}, u32[]{:S(2)}) collective-permute-start(bf16[128,512]{1,0:T(8,128)(2,1)S(1)} %get-tuple-element.188), channel_id=1, source_target_pairs={{0,128},{64,192},{128,0},{192,64},{1,129},{65,193},{129,1},{193,65... | collective-permute-start | bytes 393224 | tf_op jit(solution)/shard_map/ppermute | solution.py:20
  224.1 8.5 %collective-permute-start.60 = (bf16[128,512]{1,0:T(8,128)(2,1)S(1)}, bf16[128,512]{1,0:T(8,128)(2,1)S(1)}, u32[]{:S(2)}, u32[]{:S(2)}) collective-permute-start(bf16[128,512]{1,0:T(8,128)(2,1)S(1)} %get-tuple-element.187), channel_id=1, source_target_pairs={{0,64},{64,128},{128,192},{192,0},{1,65},{65,129},{129,193},{193,1... | collective-permute-start | bytes 393224 | tf_op jit(solution)/shard_map/ppermute | solution.py:20
  236.6 5.4 %collective-permute-start.62 = (f32[16,512]{1,0:T(8,128)S(1)}, f32[16,512]{1,0:T(8,128)S(1)}, u32[]{:S(2)}, u32[]{:S(2)}) collective-permute-start(f32[16,512]{1,0:T(8,128)S(1)} %pad_maximum_fusion.13), channel_id=1, source_target_pairs={{0,2},{1,3},{2,0},{3,1},{4,6},{5,7},{6,4},{7,5},{8,10},{9,11},{10,... | collective-permute-start | bytes 98312 | tf_op jit(solution)/shard_map/ppermute | solution.py:20
  242.1 7.0 %collective-permute-start.69 = (f32[16,512]{1,0:T(8,128)S(1)}, f32[16,512]{1,0:T(8,128)S(1)}, u32[]{:S(2)}, u32[]{:S(2)}) collective-permute-start(f32[16,512]{1,0:T(8,128)S(1)} %add_add_fusion.1), channel_id=1, source_target_pairs={{0,8},{8,16},{16,24},{24,0},{1,9},{9,17},{17,25},{25,1},{2,10},{10... | collective-permute-start | bytes 98312 | tf_op jit(solution)/shard_map/ppermute | solution.py:20
  242.8 6.5 %collective-permute-start.70 = (f32[16,512]{1,0:T(8,128)S(1)}, f32[16,512]{1,0:T(8,128)S(1)}, u32[]{:S(2)}, u32[]{:S(2)}) collective-permute-start(f32[16,512]{1,0:T(8,128)S(1)} %add_add_fusion.1), channel_id=1, source_target_pairs={{0,24},{8,0},{16,8},{24,16},{1,25},{9,1},{17,9},{25,17},{2,26},{10... | collective-permute-start | bytes 98312 | tf_op jit(solution)/shard_map/ppermute | solution.py:20
  244.2 5.4 %collective-permute-start.68 = (f32[16,512]{1,0:T(8,128)S(1)}, f32[16,512]{1,0:T(8,128)S(1)}, u32[]{:S(2)}, u32[]{:S(2)}) collective-permute-start(f32[16,512]{1,0:T(8,128)S(1)} %add_add_fusion.1), channel_id=1, source_target_pairs={{0,16},{8,24},{16,0},{24,8},{1,17},{9,25},{17,1},{25,9},{2,18},{10... | collective-permute-start | bytes 98312 | tf_op jit(solution)/shard_map/ppermute | solution.py:20
  247.0 5.8 %collective-permute-start.66 = (bf16[2,32,512]{2,1,0:T(8,128)(2,1)S(1)}, bf16[2,32,512]{2,1,0:T(8,128)(2,1)S(1)}, u32[]{:S(2)}, u32[]{:S(2)}) collective-permute-start(bf16[2,32,512]{2,1,0:T(8,128)(2,1)S(1)} %get-tuple-element.201), channel_id=1, source_target_pairs={{0,16},{8,24},{16,0},{24,8},{1,17},{9,25},{17,1},{25,9},{2,18},{10... | collective-permute-start | bytes 196616 | tf_op jit(solution)/shard_map/ppermute | solution.py:20
  249.1 5.5 %collective-permute-start.65 = (bf16[2,32,512]{2,1,0:T(8,128)(2,1)S(1)}, bf16[2,32,512]{2,1,0:T(8,128)(2,1)S(1)}, u32[]{:S(2)}, u32[]{:S(2)}) collective-permute-start(bf16[2,32,512]{2,1,0:T(8,128)(2,1)S(1)} %get-tuple-element.200), channel_id=1, source_target_pairs={{0,24},{8,0},{16,8},{24,16},{1,25},{9,1},{17,9},{25,17},{2,26},{10... | collective-permute-start | bytes 196616 | tf_op jit(solution)/shard_map/ppermute | solution.py:20
  254.6 7.9 %collective-permute-start.71 = (f32[16,512]{1,0:T(8,128)S(1)}, f32[16,512]{1,0:T(8,128)S(1)}, u32[]{:S(2)}, u32[]{:S(2)}) collective-permute-start(f32[16,512]{1,0:T(8,128)S(1)} %add_add_fusion), channel_id=1, source_target_pairs={{0,4},{4,0},{1,5},{5,1},{2,6},{6,2},{3,7},{7,3},{8,12},{12,8},{9,1... | collective-permute-start | bytes 98312 | tf_op jit(solution)/shard_map/ppermute | solution.py:24
  263.9 14.6 %collective-permute-start.76 = (bf16[224,2048]{1,0:T(8,128)(2,1)}, bf16[224,2048]{1,0:T(8,128)(2,1)S(1)}, u32[]{:S(2)}, u32[]{:S(2)}) collective-permute-start(bf16[224,2048]{1,0:T(8,128)(2,1)} %get-tuple-element.169), channel_id=1, source_target_pairs={{0,32},{32,0},{1,33},{33,1},{2,34},{34,2},{3,35},{35,3},{4,36},{36... | collective-permute-start | bytes 2752520 | tf_op jit(solution)/shard_map/ppermute | solution.py:24
  264.4 14.1 %collective-permute-start.77 = (bf16[224,2048]{1,0:T(8,128)(2,1)S(1)}, bf16[224,2048]{1,0:T(8,128)(2,1)S(1)}, u32[]{:S(2)}, u32[]{:S(2)}) collective-permute-start(bf16[224,2048]{1,0:T(8,128)(2,1)S(1)} %copy-done.31), channel_id=1, source_target_pairs={{0,32},{32,0},{1,33},{33,1},{2,34},{34,2},{3,35},{35,3},{4,36},{36... | collective-permute-start | bytes 2752520 | tf_op jit(solution)/shard_map/ppermute | solution.py:24
  264.5 14.0 %collective-permute-start.78 = (bf16[224,2048]{1,0:T(8,128)(2,1)}, bf16[224,2048]{1,0:T(8,128)(2,1)S(1)}, u32[]{:S(2)}, u32[]{:S(2)}) collective-permute-start(bf16[224,2048]{1,0:T(8,128)(2,1)} %get-tuple-element.173), channel_id=1, source_target_pairs={{0,32},{32,0},{1,33},{33,1},{2,34},{34,2},{3,35},{35,3},{4,36},{36... | collective-permute-start | bytes 2752520 | tf_op jit(solution)/shard_map/ppermute | solution.py:24
  265.7 5.7 %collective-permute-start.74 = (f32[8,128]{1,0:T(8,128)S(1)}, f32[8,128]{1,0:T(8,128)S(1)}, u32[]{:S(2)}, u32[]{:S(2)}) collective-permute-start(f32[8,128]{1,0:T(8,128)S(1)} %broadcast_add_fusion), channel_id=1, source_target_pairs={{0,64},{64,128},{128,192},{192,0},{1,65},{65,129},{129,193},{193,1... | collective-permute-start | bytes 12296 | tf_op jit(solution)/shard_map/ppermute | solution.py:20
  (49 other events, 659.5 us)
